TPU v7x, 512 devices: a whole 4x4x16 slice. The times are simulated.
512 devices in a mesh: tensor: 32 (over y, x, core), replica: 16 (over z).
Axes of the slice: x: 4, y: 4, z: 16, core: 2. Of those that a mesh axis runs over, the one named last changes fastest.
Arguments:
- hidden_in: bfloat16 [12288, 4096], P(('replica', 'tensor')), parts along dimension 0, may hold values from -6 to 6
- query_weight: bfloat16 [4096, 8192], P('tensor'), as said below
- key_weight: bfloat16 [4096, 1024], P('tensor'), as said below
- value_projection_weight: bfloat16 [4096, 1024], P('tensor'), may hold values from -0.09375 to 0.09375
- output_weight: bfloat16 [8192, 4096], P('tensor'), may hold values from -0.5 to 0.5
- head_order: int32 [64], replicated, may hold values from 0 to 63, each once
- positions: int32 [12288], P('replica'), parts along dimension 0, may hold values from 0 to 383, as said below
Outputs:
- attended: bfloat16 [12288, 4096], P(('replica', 'tensor')), parts along dimension 0
There are 16 independent parts, one for each index of `replica`. A program takes and returns all parts, laid end to end along the dimension named above; an argument that names none is the same for every part. Nothing has to cross between parts.
Inputs may be any that keep to these rules, and one draw needn't show every extreme that they name: `head_order`: each of 0 to 63 appears once. `positions`: each token's position counts up from 0 at the start of its document; token 0 starts a document. `query_weight`: finite projection weights. `key_weight`: finite projection weights.
All inputs are finite; a program needn't handle non-finite values.
Results may differ from a plain program's by a relative error of at most 0.02.
Values may be sent and summed in bfloat16 or wider, within the bound.
A program may use at most 64 MiB of HBM per device.

v0:
```python
import jax
import jax.numpy as jnp
from jax import lax
from jax.sharding import PartitionSpec as P

HEAD_SIZE = 128


rope_base = 1000000.0


def rotate_pairs(values_in, positions):
    half_width = values_in.shape[-1] // 2
    frequency = rope_base ** (
        -2.0 * jnp.arange(half_width, dtype=jnp.float32) / values_in.shape[-1]
    )
    angles = positions.astype(jnp.float32)[:, None] * frequency[None, :]
    cosine = jnp.cos(angles)[:, None, :]
    sine_part = jnp.sin(angles)[:, None, :]
    front_half = values_in[..., :half_width]
    back_half = values_in[..., half_width:]
    return jnp.concatenate(
        [front_half * cosine - back_half * sine_part, back_half * cosine + front_half * sine_part],
        axis=-1,
    )


def shards(
    hidden_in,
    query_weight,
    key_weight,
    value_projection_weight,
    output_weight,
    head_order,
    positions,
):
    devices_n = lax.axis_size("tensor")
    shard_rows = query_weight.shape[0]
    heads_all = query_weight.shape[1] // HEAD_SIZE
    kv_all = key_weight.shape[1] // HEAD_SIZE
    group_size = heads_all // kv_all
    local_heads = heads_all // devices_n
    span_len = positions.shape[0]
    inverse = jnp.argsort(head_order)
    query_cols = jnp.take(query_weight.reshape(shard_rows, heads_all, HEAD_SIZE), inverse, axis=1)
    dest_groups = jnp.arange(devices_n, dtype=jnp.int32) * local_heads // group_size
    key_sel = jnp.take(key_weight.reshape(shard_rows, kv_all, HEAD_SIZE), dest_groups, axis=1)
    value_sel = jnp.take(
        value_projection_weight.reshape(shard_rows, kv_all, HEAD_SIZE), dest_groups, axis=1
    )
    joined_cols = jnp.concatenate(
        [
            query_cols.reshape(shard_rows, devices_n, local_heads, HEAD_SIZE),
            key_sel[:, :, None, :],
            value_sel[:, :, None, :],
        ],
        axis=2,
    )
    joined_cols = joined_cols.reshape(shard_rows, devices_n * (local_heads + 2) * HEAD_SIZE)
    columns = lax.all_to_all(joined_cols, "tensor", split_axis=1, concat_axis=0, tiled=True)
    projected = jnp.dot(
        lax.all_gather(hidden_in, "tensor", axis=0, tiled=True),
        columns,
        preferred_element_type=jnp.float32,
    )
    projected = projected.reshape(span_len, local_heads + 2, HEAD_SIZE)
    query_raw = projected[:, :local_heads]
    key_one = projected[:, local_heads : local_heads + 1].astype(jnp.bfloat16)
    value_one = projected[:, local_heads + 1 : local_heads + 2].astype(jnp.bfloat16)
    key_unprojected = jnp.broadcast_to(key_one, (span_len, local_heads, HEAD_SIZE))
    value_token_rows = jnp.broadcast_to(value_one, (span_len, local_heads, HEAD_SIZE))
    queries = rotate_pairs(query_raw, positions).astype(jnp.bfloat16)
    keys = rotate_pairs(key_unprojected.astype(jnp.float32), positions).astype(jnp.bfloat16)
    scores = jnp.einsum(
        "qhd,khd->hqk", queries, keys, preferred_element_type=jnp.float32
    ) * HEAD_SIZE ** (-0.5)
    causal = jnp.arange(span_len)[:, None] >= jnp.arange(span_len)[None, :]
    scores = jnp.where(causal[None, :, :], scores, -jnp.inf)
    top_score = jnp.max(scores, axis=2, keepdims=True)
    expo_scores = jnp.exp(scores - top_score)
    probs = (expo_scores / jnp.sum(expo_scores, axis=2, keepdims=True)).astype(jnp.bfloat16)
    head_out = jnp.einsum(
        "hqk,khd->qhd", probs, value_token_rows, preferred_element_type=jnp.float32
    )
    head_out = head_out.astype(jnp.bfloat16).reshape(span_len, local_heads * HEAD_SIZE)
    return lax.psum_scatter(
        jnp.dot(head_out, output_weight, preferred_element_type=jnp.float32).astype(jnp.bfloat16),
        "tensor",
        scatter_dimension=0,
        tiled=True,
    )


def solution(mesh):
    return jax.shard_map(
        shards,
        mesh=mesh,
        in_specs=(
            P(("replica", "tensor"), None),
            P("tensor", None),
            P("tensor", None),
            P("tensor", None),
            P("tensor", None),
            P(),
            P("replica"),
        ),
        out_specs=P(("replica", "tensor"), None),
        check_vma=False,
    )
```

profile of v0, /device:TPU:1, one launch (start us, length us, event | category | flops | bytes accessed | tf_op | source)
XLA Modules:
  0.0 255.0 jit_solution(4997973235126856948)
XLA Ops:
  6.5 0.0 copy-start
  6.5 0.0 all-gather.2.cloned.1.call-start
  6.5 0.7 all-gather.2.cloned.1.call-update
  7.3 1.1 copy.29
  8.4 0.2 copy.30
  8.6 1.1 copy.31
  9.7 0.2 copy.32
  9.9 1.7 gather_fusion.1
  11.6 1.7 gather_fusion.2
  13.2 0.0 copy-start.5
  13.2 4.1 %copy.27 = bf16[128,8192]{0,1:T(8,128)(2,1)} copy(bf16[128,8192]{1,0:T(8,128)(2,1)} %param.10) | data formatting | bytes 4194304 | tf_op args[1]
  17.4 0.0 copy-start.2
  17.4 4.1 %copy.28 = bf16[128,64,128]{2,0,1:T(8,128)(2,1)} copy(bf16[128,64,128]{0,2,1:T(8,128)(2,1)} %bitcast.44) | data formatting | bytes 4194304 | tf_op jit(solution)/shard_map/reshape | solution.py:45
  21.5 0.0 copy-done.5
  21.5 2.0 sort.17
  23.5 0.1 broadcast_in_dim.68
  23.7 3.7 %gather_fusion = bf16[64,128,128]{2,1,0:T(8,128)(2,1)} fusion(bf16[128,64,128]{2,0,1:T(8,128)(2,1)} %copy.28, s32[1024]{0:T(1024)S(1)} %pad_clamp_fusion.1), kind=kCustom, calls=%fused_computation.2 | custom fusion | bytes 4194560 | tf_op jit(solution)/shard_map/jit(_take)/gather | solution.py:45
  27.4 0.0 copy-start.1
  27.5 0.0 copy-done.2
  27.5 1.6 select_bitcast_fusion.1
  29.1 0.3 copy-done.1
  29.3 0.3 broadcast_select_fusion
  29.6 2.4 copy_bitcast_fusion
  32.0 0.0 copy-start.4
  32.0 11.5 %all-to-all-start = ((bf16[128,32,512]{2,0,1:T(8,128)(2,1)}), bf16[128,32,512]{2,0,1:T(8,128)(2,1)}, u32[]{:S(2)}, u32[]{:S(2)}) async-start(bf16[128,32,512]{2,0,1:T(8,128)(2,1)} %copy_bitcast_fusion), calls=%async_computation | async-start | bytes 8388608 | tf_op jit(solution)/shard_map/all_to_all | solution.py:60
  43.5 0.0 reduce-scatter.2.cloned.1.call-start
  43.6 0.0 copy-done.4
  43.6 1.0 iota_compare_fusion
  44.6 61.9 %all-to-all-done = bf16[128,32,512]{2,0,1:T(8,128)(2,1)} async-done(((bf16[128,32,512]{2,0,1:T(8,128)(2,1)}), bf16[128,32,512]{2,0,1:T(8,128)(2,1)}, u32[]{:S(2)}, u32[]{:S(2)}) %all-to-all-start) | async-done | bytes 4194336 | tf_op jit(solution)/shard_map/all_to_all | solution.py:60
  106.6 0.4 all-gather.2.cloned.1.call-done
  106.9 7.1 %fusion.20 = f32[512,768]{1,0:T(8,128)S(1)} fusion(bf16[4096,512]{1,0:T(8,128)(2,1)} %bitcast.12, bf16[768,4096]{1,0:T(8,128)(2,1)} %all-gather.2.cloned.1.call-done), kind=kOutput, calls=%fused_computation.51 | convolution fusion | flops 3221225472 | bytes 12058624 | tf_op jit(solution)/shard_map/dot_general | solution.py:61
  114.1 0.1 convert.19
  114.2 0.9 fusion.18
  115.1 0.7 slice_bitcast_fusion.1
  115.8 1.5 multiply_cosine_fusion
  117.3 0.2 copy.37
  117.5 0.9 copy.39
  118.4 1.3 copy.44
  119.6 2.2 copy.45
  121.8 1.1 copy.40
  122.9 1.7 copy.41
  124.6 2.3 subtract_convert_fusion
  126.9 1.0 broadcast_in_dim.78
  127.9 0.0 copy-start.3
  127.9 5.5 %fusion.19 = (f32[2,768]{1,0:T(2,128)S(1)}, f32[2,768,768]{1,2,0:T(8,128)}) fusion(pred[768,768]{0,1:T(8,128)(4,1)} %iota_compare_fusion, bf16[768,2,64]{2,0,1:T(8,128)(2,1)S(1)} %broadcast_in_dim.78, bf16[768,2,64]{2,0,1:T(8,128)(2,1)S(1)} %broadcast_in_dim.77, bf16[768,2,64]{2,0,1:T(8,128)(2,1)} %get-tuple-element.9, bf16[768,2,64]{2,0,1:T(8,128)(2,1)} %get-tuple-element.8), kind=kOutput, calls=%fused_computation.50 | convolution fusion | flops 308282112 | bytes 6100992 | tf_op jit(solution)/shard_map/sub | solution.py:80
  133.4 0.0 copy-done.3
  133.4 2.8 %fusion.6 = bf16[2,128,768]{2,1,0:T(8,128)(2,1)S(1)} fusion(f32[2,768,768]{1,2,0:T(8,128)} %get-tuple-element.23, f32[2,768]{1,0:T(2,128)S(1)} %get-tuple-element.22, bf16[768,128]{0,1:T(8,128)(2,1)S(1)} %copy-done.3), kind=kOutput, calls=%fused_computation.17 | convolution fusion | flops 304545792 | bytes 5314560 | tf_op jit(solution)/shard_map/hqk,khd->qhd/dot_general | solution.py:82
  136.2 0.0 copy-done
  136.3 4.5 %convolution_convert_fusion = bf16[768,4096]{1,0:T(8,128)(2,1)} fusion(bf16[768,256]{0,1:T(8,128)(2,1)S(1)} %bitcast.49, bf16[256,4096]{1,0:T(8,128)(2,1)S(1)} %copy-done), kind=kOutput, calls=%fused_computation.4 | convolution fusion | flops 1613758464 | bytes 8781824 | tf_op jit(solution)/shard_map/dot_general | solution.py:87
  140.7 0.0 reduce-scatter.2.cloned.1.call-update
  140.8 107.3 %reduce-scatter.2.cloned.1.call-done = bf16[24,4096]{1,0:T(8,128)(2,1)} async-done(((bf16[768,4096]{1,0:T(8,128)(2,1)}), bf16[24,4096]{1,0:T(8,128)(2,1)}) %reduce-scatter.2.cloned.1.call-update) | async-done | bytes 196624 | tf_op jit(solution)/shard_map/reduce_scatter | solution.py:86
  (10 shorter events, 0.1 us)
Async XLA Ops:
  6.5 129.7 %copy-start = (bf16[256,4096]{1,0:T(8,128)(2,1)S(1)}, bf16[256,4096]{1,0:T(8,128)(2,1)}, u32[]{:S(2)}) copy-start(bf16[256,4096]{1,0:T(8,128)(2,1)} %param.13) | copy-start | bytes 6291460
  6.5 100.4 %all-gather.2.cloned.1.call-start = ((), (), s32[]{:S(2)}) async-start(), calls=%async_computation.2 | async-start | bytes 6488064 | tf_op jit(solution)/shard_map/all_gather | solution.py:62
  13.2 8.3 %copy-start.5 = (s32[64]{0:T(128)S(1)}, s32[64]{0:T(128)}, u32[]{:S(2)}) copy-start(s32[64]{0:T(128)} %param.14) | copy-start | bytes 772
  17.4 10.1 %copy-start.2 = (bf16[32,128,128]{2,1,0:T(8,128)(2,1)S(1)}, bf16[32,128,128]{2,1,0:T(8,128)(2,1)}, u32[]{:S(2)}) copy-start(bf16[32,128,128]{2,1,0:T(8,128)(2,1)} %gather_fusion.1) | copy-start | bytes 3145732
  27.4 1.9 copy-start.1
  32.0 11.6 %copy-start.4 = (s32[768]{0:T(1024)S(1)}, s32[768]{0:T(1024)}, u32[]{:S(2)}) copy-start(s32[768]{0:T(1024)} %param.15) | copy-start | bytes 9220
  32.0 74.6 %all-to-all-start = ((bf16[128,32,512]{2,0,1:T(8,128)(2,1)}), bf16[128,32,512]{2,0,1:T(8,128)(2,1)}, u32[]{:S(2)}, u32[]{:S(2)}) async-start(bf16[128,32,512]{2,0,1:T(8,128)(2,1)} %copy_bitcast_fusion), calls=%async_computation | async-start | bytes 8388608 | tf_op jit(solution)/shard_map/all_to_all | solution.py:60
  43.5 204.6 %reduce-scatter.2.cloned.1.call-start = ((), (), s32[]{:S(2)}) async-start(), calls=%async_computation.3 | async-start | bytes 6488064 | tf_op jit(solution)/shard_map/reduce_scatter | solution.py:86
  127.9 5.5 %copy-start.3 = (bf16[768,128]{0,1:T(8,128)(2,1)S(1)}, bf16[768,128]{0,1:T(8,128)(2,1)}, u32[]{:S(2)}) copy-start(bf16[768,128]{0,1:T(8,128)(2,1)} %get-tuple-element.12) | copy-start | bytes 589828
Sparse Core Ops, SparseCore 0:
  10.5 96.3 all-gather.1
  140.9 107.1 reduce-scatter.1
where the time goes:
time: 256 us; the launch traced here: 255 us
  waiting for transfers between devices  170 us (66%)
  local copies, waits for them, and re-layouts  27.5 us (11%)
  matrix products  19.9 us (8%)
  between operations  13.6 us (5%)
  other arithmetic  12 us (5%)
  starting transfers between devices  11.6 us (5%)
    reduce_scatter x1, waiting for transfers between devices, shards(): lax.psum_scatter(jnp.dot(head_out, output_weight, preferred_element_type=...  107 us
    all_to_all x1, waiting for transfers between devices, shards(): lax.all_to_all(joined_cols, 'tensor', split_axis=1, concat_axis=0, tiled=...  61.9 us
    all_to_all x1, starting transfers between devices, shards(): lax.all_to_all(joined_cols, 'tensor', split_axis=1, concat_axis=0, tiled=...  11.5 us
    unnamed x17, local copies, waits for them, and re-layouts  10.1 us
    dot_general x1, matrix products, shards(): jnp.dot(lax.all_gather(hidden_in, 'tensor', axis=0, tiled=True), columns,...  7.13 us
    sub x1, matrix products, shards(): expo_scores = jnp.exp(scores - top_score)  5.49 us
  transfers between devices with their start and end apart: 3, of which 3 were waited for; matrix products, arithmetic and copies ran while one was open for 10% of the time, Pallas kernels for 0%

commit v1 on v0

v1 whole, which is shorter than its diff:
```python
import math

import jax
import jax.numpy as jnp
import numpy as np
from jax import lax
from jax.experimental import pallas as pl
from jax.experimental.pallas import tpu as pltpu
from jax.sharding import PartitionSpec as P

MESH = pl.DeviceIdType.MESH
F32, BF16 = jnp.float32, jnp.bfloat16

HEAD = 128
RING = 4
TOK = 48
ROWS = RING * TOK
SPAN = RING * ROWS
FEAT = 4096
DEPTH = FEAT // RING
KV_COLS = RING * HEAD
Q_COLS = RING * 2 * HEAD
HALF = FEAT // 2
ROPE_BASE = 1000000.0
EXP_SCALE = math.log2(math.e) / math.sqrt(HEAD)


def kernel(
    x_hbm, wq_hbm, wk_hbm, wv_hbm, wo_hbm, inv_ref, ang_ref,
    out_ref,
    xpair, xs, xall, wq, wkv, wsend, wall, wo2, cos_t, sin_t,
    ykv, ykv_in, yq, yq_in, kv, hbuf, obuf, o1_in, o1_sum, o2_in, fin_out, fin_in,
    loc_sem, d2d_s, d2d_r, w_s, w_r, x1_s, x2_s, x_r, ykv_s, ykv_r, yq_s, yq_r,
    h_s, h_r, o1_s, o1_r, o2_s, o2_r,
):
    t = lax.axis_index("tensor")
    y, x, c = t // 8, (t // 2) % 4, t % 2
    first = c == 0
    p, s = jnp.where(first, x, y), jnp.where(first, y, x)
    oc = 1 - c

    def wrap(v):
        return lax.rem(v + 8, RING)

    def device(pp, ss):
        return jnp.where(first, 8 * ss + 2 * pp, 8 * pp + 2 * ss + 1)

    def slot(pp, ss):
        yy, xx = jnp.where(first, ss, pp), jnp.where(first, pp, ss)
        return RING * wrap(xx - yy) + yy

    def remote(src, dst, ss, rs, dev):
        return pltpu.make_async_remote_copy(
            src_ref=src, dst_ref=dst, send_sem=ss, recv_sem=rs,
            device_id={"tensor": dev}, device_id_type=MESH,
        )

    partner = t + 1 - 2 * c

    own_x = pltpu.make_async_copy(x_hbm, xpair.at[c], loc_sem.at[0])
    own_q = pltpu.make_async_copy(wq, wq, loc_sem.at[1])
    own_k = pltpu.make_async_copy(wk_hbm, wkv.at[0], loc_sem.at[2])
    own_v = pltpu.make_async_copy(wv_hbm, wkv.at[1], loc_sem.at[3])
    own_o = pltpu.make_async_copy(
        wo_hbm.at[:, pl.ds(pl.multiple_of(c * HALF, HALF), HALF)], wo2.at[c], loc_sem.at[4]
    )

    def load_head(i, _):
        cols = pl.ds(pl.multiple_of(i * HEAD, HEAD), HEAD)
        pltpu.make_async_copy(wq_hbm.at[:, cols], wq.at[i], loc_sem.at[1]).start()
        return 0

    own_k.start()
    own_v.start()
    lax.fori_loop(0, 64, load_head, 0)
    own_x.start()
    own_o.start()

    barrier = pltpu.get_barrier_semaphore()

    def greet(dev):
        pl.semaphore_signal(barrier, inc=1, device_id={"tensor": dev}, device_id_type=MESH)

    greet(partner)
    for d in range(1, RING):
        ring = device(wrap(p + d), s)
        greet(ring)
        greet(ring + 1 - 2 * c)
        greet(device(p, wrap(s + d)))
    pl.semaphore_wait(barrier, 10)

    x_d2d = remote(x_hbm, xpair.at[c], d2d_s.at[0], d2d_r.at[0], partner)
    x_d2d.start()

    own_q.wait()
    own_k.wait()
    own_v.wait()
    w_copies = []
    for other in (0, 1):
        cc = jnp.where(other == 1, oc, c)
        cc_first = cc == 0
        pcc = jnp.where(cc_first, x, y)
        for d in (1, 2, 3, 0):
            pp = wrap(pcc + d)
            own = other == 0 and d == 0
            place = wall.at[2 * p + c] if own else wsend.at[RING * other + d]

            def fill(ss, _, place=place, cc=cc, cc_first=cc_first, pp=pp):
                tt = jnp.where(cc_first, 8 * ss + 2 * pp, 8 * pp + 2 * ss + 1)
                group = pl.multiple_of((tt // 4) * HEAD, HEAD)
                place[:, pl.ds(pl.multiple_of(ss * HEAD, HEAD), HEAD)] = wkv[
                    cc, :, pl.ds(group, HEAD)
                ]
                for i in range(2):
                    at = pl.multiple_of(KV_COLS + (2 * ss + i) * HEAD, HEAD)
                    place[:, pl.ds(at, HEAD)] = wq[inv_ref[2 * tt + i]]
                return 0

            lax.fori_loop(0, RING, fill, 0)
            if not own:
                dev = jnp.where(cc_first, 8 * y + 2 * pp, 8 * pp + 2 * x + 1)
                copy = remote(
                    place, wall.at[2 * pcc + c],
                    w_s.at[RING * other + d], w_r.at[2 * pcc + c], dev,
                )
                copy.start()
                w_copies.append(copy)

    own_x.wait()
    x_d2d.wait_send()
    remote(x_hbm, xpair.at[oc], d2d_s.at[0], d2d_r.at[0], partner).wait_recv()
    wo_d2d = remote(
        wo_hbm.at[:, pl.ds(pl.multiple_of(oc * HALF, HALF), HALF)], wo2.at[c],
        d2d_s.at[1], d2d_r.at[1], partner,
    )
    wo_d2d.start()
    mine = slot(p, s)
    x_copies = []
    for d in (1, 2, 3, 0):
        ss = wrap(s + d)
        for pp in range(RING):
            feat = pl.multiple_of(
                jnp.where(first, DEPTH * ss + 256 * pp, DEPTH * pp + 256 * ss), 256
            )
            rows = jnp.concatenate(
                [xpair[0, :, pl.ds(feat, 256)].astype(F32), xpair[1, :, pl.ds(feat, 256)].astype(F32)],
                axis=0,
            ).astype(BF16)
            if d == 0:
                xall[mine, :, 256 * pp : 256 * pp + 256] = rows
            else:
                xs[d, :, 256 * pp : 256 * pp + 256] = rows
        if d:
            copy = remote(xs.at[d], xall.at[mine], x1_s.at[d], x_r.at[mine], device(p, ss))
            copy.start()
            x_copies.append(copy)

    def arrived(m):
        remote(xall.at[m], xall.at[m], x1_s.at[0], x_r.at[m], partner).wait_recv()

    for d in range(RING):
        m = slot(p, wrap(s + d))
        if d:
            arrived(m)
        for e in (1, 2, 3):
            copy = remote(
                xall.at[m], xall.at[m], x2_s.at[RING * e + d], x_r.at[m], device(wrap(p + e), s)
            )
            copy.start()
            x_copies.append(copy)

    sign = jnp.where(lax.broadcasted_iota(jnp.int32, (TOK, HEAD), 1) < HEAD // 2, -1.0, 1.0)

    def table(n, _):
        at = pl.ds(pl.multiple_of(n * TOK, TOK), TOK)
        ang = ang_ref[at, :]
        cos_t[at, :] = jnp.cos(ang)
        sin_t[at, :] = jnp.sin(ang) * sign
        return 0

    lax.fori_loop(0, RING * RING, table, 0)

    own_o.wait()
    wo_d2d.wait()
    for e in range(RING):
        for cs in range(2):
            k = 2 * wrap(p + e) + (c if cs == 0 else oc)
            if e or cs:
                remote(wall.at[k], wall.at[k], w_s.at[0], w_r.at[k], partner).wait_recv()
    for e in (1, 2, 3):
        for ss in range(RING):
            arrived(slot(wrap(p + e), ss))

    def tokens(j):
        return xall[pl.ds(j * RING, RING)].reshape(ROWS, DEPTH)

    def partial_kv(j, _):
        r = jnp.dot(
            tokens(j), wall[:, :, :KV_COLS].reshape(DEPTH, KV_COLS), preferred_element_type=F32
        ).astype(BF16)
        at = pl.ds(pl.multiple_of(j * ROWS, ROWS), ROWS)
        for ss in range(RING):
            ykv[ss, at, :] = r[:, ss * HEAD : (ss + 1) * HEAD]
        return 0

    lax.fori_loop(0, RING, partial_kv, 0)
    y_copies = []
    for d in (2, 1, 3):
        ss = wrap(s + d)
        copy = remote(ykv.at[ss], ykv_in.at[s], ykv_s.at[d], ykv_r.at[s], device(p, ss))
        copy.start()
        y_copies.append(copy)
    for j in range(RING):
        r = jnp.dot(
            tokens(j), wall[:, :, KV_COLS:].reshape(DEPTH, Q_COLS), preferred_element_type=F32
        ).astype(BF16)
        for ss in range(RING):
            yq[j, ss] = r[:, ss * 2 * HEAD : (ss + 1) * 2 * HEAD]
        for d in (2, 1, 3):
            ss = wrap(s + d)
            copy = remote(
                yq.at[j, ss], yq_in.at[j, s], yq_s.at[j, d], yq_r.at[j, s], device(p, ss)
            )
            copy.start()
            y_copies.append(copy)

    def rotate(v, at):
        return v * cos_t[at, :] + pltpu.roll(v, HEAD // 2, 1) * sin_t[at, :]

    def place_of(j, b):
        return RING * b + (b + j) % RING

    for d in (1, 2, 3):
        ss = wrap(s + d)
        remote(ykv.at[ss], ykv_in.at[ss], ykv_s.at[d], ykv_r.at[ss], partner).wait_recv()
    for j in range(RING):
        for b in range(RING):
            rows = pl.ds((RING * j + b) * TOK, TOK)
            at = pl.ds(place_of(j, b) * TOK, TOK)
            total = ykv[s, rows, :].astype(F32)
            for d in (1, 2, 3):
                total += ykv_in[wrap(s + d), rows, :].astype(F32)
            whole = total.astype(BF16)
            kv[c, at, :] = jnp.where(first, rotate(whole.astype(F32), at), whole.astype(F32)).astype(BF16)
    kv_d2d = remote(kv.at[c], kv.at[c], d2d_s.at[2], d2d_r.at[2], partner)
    kv_d2d.start()
    remote(kv.at[oc], kv.at[oc], d2d_s.at[2], d2d_r.at[2], partner).wait_recv()

    h_copies, o_copies = [], []

    def attend(j):
        for d in (1, 2, 3):
            ss = wrap(s + d)
            remote(yq.at[j, ss], yq_in.at[j, ss], yq_s.at[j, d], yq_r.at[j, ss], partner).wait_recv()
        for b in range(RING):
            n = place_of(j, b)
            rows, at = pl.ds(b * TOK, TOK), pl.ds(n * TOK, TOK)
            total = yq[j, s, rows, :].astype(F32)
            for d in (1, 2, 3):
                total += yq_in[j, wrap(s + d), rows, :].astype(F32)
            q = jnp.concatenate(
                [rotate(total[:, :HEAD], at), rotate(total[:, HEAD:], at)], axis=0
            ).astype(BF16)
            keys = -(-(n + 1) * TOK // HEAD) * HEAD
            scores = lax.dot_general(
                q, kv[0, :keys, :], (((1,), (1,)), ((), ())), preferred_element_type=F32
            )
            row = lax.broadcasted_iota(jnp.int32, (2 * TOK, keys), 0)
            row = jnp.where(row >= TOK, row - TOK, row) + n * TOK
            col = lax.broadcasted_iota(jnp.int32, (2 * TOK, keys), 1)
            scores = jnp.where(col <= row, scores, -jnp.inf)
            top = jnp.max(scores, axis=1, keepdims=True)
            expo = jnp.exp2((scores - top) * EXP_SCALE)
            norm = jnp.sum(expo, axis=1, keepdims=True)
            head = jnp.dot(expo.astype(BF16), kv[1, :keys, :], preferred_element_type=F32) / norm
            hbuf[c, j, rows, :] = jnp.concatenate([head[:TOK], head[TOK:]], axis=1).astype(BF16)
        copy = remote(hbuf.at[c, j], hbuf.at[c, j], h_s.at[j], h_r.at[j], partner)
        copy.start()
        h_copies.append(copy)

    def project(j):
        remote(hbuf.at[oc, j], hbuf.at[oc, j], h_s.at[j], h_r.at[j], partner).wait_recv()
        r = jnp.dot(hbuf[0, j], wo2[0], preferred_element_type=F32)
        r += jnp.dot(hbuf[1, j], wo2[1], preferred_element_type=F32)
        obuf[j] = r.astype(BF16).reshape(RING, TOK, HALF)
        for d in (2, 1, 3):
            pp = wrap(p + d)
            b = jnp.where(first, wrap(pp - j), pp)
            copy = remote(
                obuf.at[j, b], o1_in.at[j, p], o1_s.at[j, d], o1_r.at[j, p], device(pp, s)
            )
            copy.start()
            o_copies.append(copy)

    def target(j):
        return jnp.where(first, wrap(p - j), wrap(p + j))

    def second(j):
        ss = target(j)
        return remote(o1_sum.at[j], o2_in.at[s], o2_s.at[j], o2_r.at[s], device(p, ss))

    def combine(j):
        total = obuf[j, jnp.where(first, wrap(p - j), p)].astype(F32)
        for d in (1, 2, 3):
            pp = wrap(p + d)
            remote(obuf.at[j, 0], o1_in.at[j, pp], o1_s.at[j, d], o1_r.at[j, pp], partner).wait_recv()
            total += o1_in[j, pp].astype(F32)
        o1_sum[j] = total.astype(BF16)

        @pl.when(target(j) != s)
        def _():
            second(j).start()

    attend(0)
    for j in range(1, RING):
        attend(j)
        project(j - 1)
        if j >= 2:
            combine(j - 2)
    project(RING - 1)
    combine(RING - 2)
    combine(RING - 1)

    kept = jnp.where(first, wrap(p - s), wrap(s - p))
    total = o1_sum[kept].astype(F32)
    for d in (1, 2, 3):
        ss = wrap(s + d)
        remote(o1_sum.at[0], o2_in.at[ss], o2_s.at[0], o2_r.at[ss], partner).wait_recv()
        total += o2_in[ss].astype(F32)
    low, high = total[: TOK // 2], total[TOK // 2 :]
    fin_out[...] = jnp.where(first, high, low).astype(BF16)
    fin_d2d = remote(fin_out, fin_in, d2d_s.at[3], d2d_r.at[3], partner)
    fin_d2d.start()
    out_ref[:, pl.ds(pl.multiple_of(c * HALF, HALF), HALF)] = jnp.where(first, low, high).astype(BF16)

    kv_d2d.wait_send()
    for copy in w_copies + x_copies + y_copies + h_copies + o_copies:
        copy.wait_send()
    for j in range(RING):

        @pl.when(target(j) != s)
        def _(j=j):
            second(j).wait_send()

    fin_d2d.wait()
    out_ref[:, pl.ds(pl.multiple_of(oc * HALF, HALF), HALF)] = fin_in[...]


def shards(hidden_in, query_weight, key_weight, value_projection_weight, output_weight, head_order, positions):
    heads = jnp.arange(head_order.shape[0], dtype=jnp.int32)
    inverse = jnp.sum(
        jnp.where(head_order[None, :] == heads[:, None], heads[None, :], 0), axis=1, dtype=jnp.int32
    )
    half = np.float32(ROPE_BASE) ** (
        np.float32(-2.0) * np.arange(HEAD // 2, dtype=np.float32) / np.float32(HEAD)
    )
    angles = positions.astype(F32)[:, None] * jnp.asarray(np.concatenate([half, half]))[None, :]
    vmem, dma = pltpu.VMEM, pltpu.SemaphoreType.DMA
    any_spec = pl.BlockSpec(memory_space=pl.ANY)
    vmem_spec = pl.BlockSpec(memory_space=vmem)
    return pl.pallas_call(
        kernel,
        out_shape=jax.ShapeDtypeStruct((TOK // 2, FEAT), BF16),
        in_specs=[any_spec] * 5 + [pl.BlockSpec(memory_space=pltpu.SMEM), vmem_spec],
        out_specs=vmem_spec,
        scratch_shapes=[
            vmem((2, TOK // 2, FEAT), BF16),
            vmem((RING, TOK, DEPTH), BF16),
            vmem((RING * RING, TOK, DEPTH), BF16),
            vmem((64, 128, HEAD), BF16),
            vmem((2, 128, 1024), BF16),
            vmem((2 * RING, 128, KV_COLS + Q_COLS), BF16),
            vmem((2 * RING, 128, KV_COLS + Q_COLS), BF16),
            vmem((2, 2 * HEAD, HALF), BF16),
            vmem((SPAN, HEAD), F32),
            vmem((SPAN, HEAD), F32),
            vmem((RING, SPAN, HEAD), BF16),
            vmem((RING, SPAN, HEAD), BF16),
            vmem((RING, RING, ROWS, 2 * HEAD), BF16),
            vmem((RING, RING, ROWS, 2 * HEAD), BF16),
            vmem((2, SPAN, HEAD), BF16),
            vmem((2, RING, ROWS, 2 * HEAD), BF16),
            vmem((RING, RING, TOK, HALF), BF16),
            vmem((RING, RING, TOK, HALF), BF16),
            vmem((RING, TOK, HALF), BF16),
            vmem((RING, TOK, HALF), BF16),
            vmem((TOK // 2, HALF), BF16),
            vmem((TOK // 2, HALF), BF16),
            dma((5,)), dma((4,)), dma((4,)),
            dma((2 * RING,)), dma((2 * RING,)),
            dma((RING,)), dma((RING * RING,)), dma((RING * RING,)),
            dma((RING,)), dma((RING,)), dma((RING, RING)), dma((RING, RING)),
            dma((RING,)), dma((RING,)),
            dma((RING, RING)), dma((RING, RING)), dma((RING,)), dma((RING,)),
        ],
        compiler_params=pltpu.CompilerParams(
            collective_id=0, has_side_effects=True, vmem_limit_bytes=56 << 20
        ),
        cost_estimate=pl.CostEstimate(flops=6 << 30, bytes_accessed=8 << 20, transcendentals=1 << 20),
    )(hidden_in, query_weight, key_weight, value_projection_weight, output_weight, inverse, angles)


def solution(mesh):
    return jax.shard_map(
        shards,
        mesh=mesh,
        in_specs=(
            P(("replica", "tensor"), None),
            P("tensor", None),
            P("tensor", None),
            P("tensor", None),
            P("tensor", None),
            P(),
            P("replica"),
        ),
        out_specs=P(("replica", "tensor"), None),
        check_vma=False,
    )
```

time: 256 us -> 95.3 us (0.37)
  the two profiles are of different devices: /device:TPU:1 before, /device:TPU:9 now
where the time goes in v1:
time: 95.3 us; the launch traced here: 95.1 us
  Pallas kernels  89.9 us (94%)
  other arithmetic  3.53 us (4%)
  local copies, waits for them, and re-layouts  1.62 us (2%)
    pallas_call x1, Pallas kernels, shards(): pl.pallas_call(kernel, out_shape=jax.ShapeDtypeStruct((TOK // 2, FEAT), B...  89.9 us

profile of v1, /device:TPU:9, one launch (start us, length us, event | category | flops | bytes accessed | tf_op | source)
XLA Modules:
  0.0 95.1 jit_solution(13291239824734777360)
XLA Ops:
  0.0 1.3 %select_reduce_fusion.inv_ref = s32[64]{0:T(128)} fusion(s32[64]{0:T(128)} %param.13), kind=kLoop, calls=%fused_computation.1 | loop fusion | flops 12224 | bytes 512 | tf_op jit(solution)/shard_map/reduce_sum | solution.py:351
  1.3 0.7 convert_element_type.3
  2.0 1.6 %broadcast_multiply_fusion.ang_ref = f32[768,128]{1,0:T(8,128)} fusion(f32[128]{0:T(128)} %constant.4.clone, f32[768]{0:T(1024)S(1)} %convert_element_type.3), kind=kLoop, calls=%fused_computation | loop fusion | flops 98304 | bytes 396800 | tf_op jit(solution)/shard_map/mul | solution.py:357
  3.5 89.9 %shard_map.82 = bf16[24,4096]{1,0:T(8,128)(2,1)} custom-call(bf16[24,4096]{1,0:T(8,128)(2,1)} %x_hbm.1, bf16[128,8192]{1,0:T(8,128)(2,1)} %wq_hbm.1, bf16[128,1024]{1,0:T(8,128)(2,1)} %wk_hbm.1, bf16[128,1024]{1,0:T(8,128)(2,1)} %wv_hbm.1, bf16[256,4096]{1,0:T(8,128)(2,1)} %wo_hbm.1, s32[64]{0:T(128)} %select_reduce_fusion.inv_ref, ...), custom_call_target="tpu_custom_call" | custom-call | flops 6442450944 | bytes 8388608 | tf_op jit(solution)/shard_map/pallas_call | solution.py:361
  93.5 1.6 %copy.10 = bf16[24,4096]{1,0:T(8,128)(2,1)} copy(bf16[24,4096]{1,0:T(8,128)(2,1)} %shard_map.82) | data formatting | bytes 393216

commit v2 on v1

v2 whole, which is shorter than its diff:
```python
import math

import jax
import jax.numpy as jnp
import numpy as np
from jax import lax
from jax.experimental import pallas as pl
from jax.experimental.pallas import tpu as pltpu
from jax.sharding import PartitionSpec as P

MESH = pl.DeviceIdType.MESH
F32, BF16 = jnp.float32, jnp.bfloat16

HEAD = 128
RING = 4
TOK = 48
ROWS = RING * TOK
CUT = 16
CHUNK = RING * RING * CUT
SPAN = RING * ROWS
FEAT = 4096
DEPTH = FEAT // RING
KV_COLS = RING * HEAD
Q_COLS = RING * 2 * HEAD
HALF = FEAT // 2
WIDE = HALF // 2
HEADS = 64
W_ROWS = 128
ROPE_BASE = 1000000.0
EXP_SCALE = math.log2(math.e) / math.sqrt(HEAD)


def kernel(
    x_hbm, wq_hbm, wk_hbm, wv_hbm, wo_hbm, order_ref, pos_ref, freq_ref,
    out_ref,
    xpair, xs, xall, wq, wkv, wsend, wall, wo2, inv_v, inv_s, cos_t, sin_t,
    ykv, ykv_in, yq, yq_in, kv, hbuf, obuf, f_in, o1_in, o1_sum, o2_in, fin_out, fin_in,
    loc_sem, d2d_s, d2d_r, w_s, w_r, z_s, z_r, x1_s, x2_s, x_r, ykv_s, ykv_r, yq_s, yq_r,
    kv_s, kv_r, h_s, h_r, f_s, f_r, o1_s, o1_r, o2_s, o2_r,
):
    t = lax.axis_index("tensor")
    z = lax.axis_index("replica")
    planes = lax.axis_size("replica")
    y, x, c = t // 8, (t // 2) % 4, t % 2
    first = c == 0
    p, s = jnp.where(first, x, y), jnp.where(first, y, x)
    oc = 1 - c
    part = z % 2

    def wrap(v):
        return lax.rem(v + 8, RING)

    def device(pp, ss):
        return jnp.where(first, 8 * ss + 2 * pp, 8 * pp + 2 * ss + 1)

    def slot(pp, ss):
        return jnp.where(first, RING * ss + pp, RING * pp + ss)

    def remote(src, dst, ss, rs, dev, dz=0):
        where = {"tensor": dev}
        if dz:
            where["replica"] = lax.rem(z + dz + planes, planes)
        return pltpu.make_async_remote_copy(
            src_ref=src, dst_ref=dst, send_sem=ss, recv_sem=rs,
            device_id=where, device_id_type=MESH,
        )

    partner = t + 1 - 2 * c

    barrier = pltpu.get_barrier_semaphore()

    def greet(dev, dz=0):
        where = {"tensor": dev}
        if dz:
            where["replica"] = lax.rem(z + dz + planes, planes)
        pl.semaphore_signal(barrier, inc=1, device_id=where, device_id_type=MESH)

    for d in range(1, RING):
        ring = device(wrap(p + d), s)
        greet(ring)
        greet(ring + 1 - 2 * c)
        greet(device(p, wrap(s + d)))
    greet(t, 1)
    greet(t, -1)
    greet(partner)

    own_x = pltpu.make_async_copy(x_hbm, xpair.at[c], loc_sem.at[0])
    own_q = pltpu.make_async_copy(wq, wq, loc_sem.at[1])
    own_k = pltpu.make_async_copy(wk_hbm, wkv.at[0], loc_sem.at[2])
    own_v = pltpu.make_async_copy(wv_hbm, wkv.at[1], loc_sem.at[3])
    own_o = pltpu.make_async_copy(
        wo_hbm.at[:, pl.ds(pl.multiple_of(c * HALF, HALF), HALF)], wo2.at[c], loc_sem.at[4]
    )

    def load_head(i, _):
        cols = pl.ds(pl.multiple_of(i * HEAD, HEAD), HEAD)
        pltpu.make_async_copy(wq_hbm.at[:, cols], wq.at[i], loc_sem.at[1]).start()
        return 0

    own_k.start()
    own_v.start()
    lax.fori_loop(0, HEADS, load_head, 0, unroll=8)
    own_x.start()
    own_o.start()

    lane = lax.broadcasted_iota(jnp.int32, (8, HEAD), 1)

    def invert(i, acc):
        return jnp.where(lane == order_ref[i], i, acc)

    inv_v[...] = lax.fori_loop(0, HEADS, invert, jnp.zeros((8, HEAD), jnp.int32), unroll=8)
    to_scalars = pltpu.make_async_copy(inv_v, inv_s, loc_sem.at[5])
    to_scalars.start()

    pl.semaphore_wait(barrier, 12)

    x_d2d = remote(x_hbm, xpair.at[c], d2d_s.at[0], d2d_r.at[0], partner)
    x_d2d.start()
    to_scalars.wait()
    own_k.wait()
    own_v.wait()
    own_q.wait()

    sends = []
    half_rows = W_ROWS // 2
    moved = pl.ds(pl.multiple_of(part * half_rows, half_rows), half_rows)
    brought = pl.ds(pl.multiple_of((1 - part) * half_rows, half_rows), half_rows)

    def weights(other, d):
        cc = jnp.where(other == 1, oc, c)
        cc_first = cc == 0
        pcc = jnp.where(cc_first, x, y)
        pp = wrap(pcc + d)
        own = other == 0 and d == 0
        rows = moved if d else pl.ds(0, W_ROWS)
        place = wall.at[2 * p + c] if own else wsend.at[RING * other + d]

        def fill(ss, _):
            tt = jnp.where(cc_first, 8 * ss + 2 * pp, 8 * pp + 2 * ss + 1)
            group = pl.multiple_of((tt // 4) * HEAD, HEAD)
            place[rows, pl.ds(pl.multiple_of(ss * HEAD, HEAD), HEAD)] = wkv[cc, rows, pl.ds(group, HEAD)]
            for i in range(2):
                at = pl.multiple_of(KV_COLS + (2 * ss + i) * HEAD, HEAD)
                place[rows, pl.ds(at, HEAD)] = wq[inv_s[0, 2 * tt + i], rows]
            return 0

        lax.fori_loop(0, RING, fill, 0)
        if not own:
            dev = jnp.where(cc_first, 8 * y + 2 * pp, 8 * pp + 2 * x + 1)
            copy = remote(
                place.at[rows], wall.at[2 * pcc + c, rows],
                w_s.at[RING * other + d], w_r.at[2 * pcc + c], dev,
            )
            copy.start()
            sends.append(copy)

    for d in (1, 3, 2):
        weights(0, d)

    own_x.wait()
    remote(x_hbm, xpair.at[oc], d2d_s.at[0], d2d_r.at[0], partner).wait_recv()
    mine = slot(p, s)
    for d in (1, 3, 2, 0):
        ss = wrap(s + d)
        for pp in range(RING):
            feat = pl.multiple_of(
                jnp.where(first, DEPTH * ss + 256 * pp, DEPTH * pp + 256 * ss), 256
            )
            rows = jnp.concatenate(
                [xpair[0, :, pl.ds(feat, 256)].astype(F32), xpair[1, :, pl.ds(feat, 256)].astype(F32)],
                axis=0,
            ).astype(BF16)
            if d == 0:
                xall[mine, :, 256 * pp : 256 * pp + 256] = rows
            else:
                xs[d, :, 256 * pp : 256 * pp + 256] = rows
        if d:
            copy = remote(xs.at[d], xall.at[mine], x1_s.at[d], x_r.at[mine], device(p, ss))
            copy.start()
            sends.append(copy)

    for d in (1, 3, 2):
        weights(1, d)
    weights(1, 0)
    weights(0, 0)
    x_d2d.wait_send()
    wo_d2d = remote(
        wo_hbm.at[:, pl.ds(pl.multiple_of(oc * HALF, HALF), HALF)], wo2.at[c],
        d2d_s.at[1], d2d_r.at[1], partner,
    )
    wo_d2d.start()

    def arrived(m):
        remote(xall.at[m], xall.at[m], x1_s.at[0], x_r.at[m], partner).wait_recv()

    def from_plane(e):
        for other in (0, 1):
            k = 2 * wrap(p + e) + (oc if other else c)
            here = wall.at[k, moved]
            remote(here, here, w_s.at[0], w_r.at[k], partner).wait_recv()
            copy = remote(here, here, z_s.at[k], z_r.at[k], t, -1 if other else 1)
            copy.start()
            sends.append(copy)

    def forward(d):
        m = slot(p, wrap(s + d))
        if d:
            arrived(m)
        for e in (1, 3, 2):
            copy = remote(
                xall.at[m], xall.at[m], x2_s.at[RING * e + d], x_r.at[m], device(wrap(p + e), s)
            )
            copy.start()
            sends.append(copy)

    from_plane(1)
    from_plane(3)
    for d in range(RING):
        forward(d)
    from_plane(2)

    eye = lax.broadcasted_iota(jnp.int32, (HEAD, HEAD), 0) == lax.broadcasted_iota(
        jnp.int32, (HEAD, HEAD), 1
    )
    sign = jnp.where(lax.broadcasted_iota(jnp.int32, (HEAD, HEAD), 1) < HEAD // 2, -1.0, 1.0)

    def table(n, _):
        at = pl.ds(pl.multiple_of(n * HEAD, HEAD), HEAD)
        line = pos_ref[at].astype(F32)
        column = jnp.sum(jnp.where(eye, line[None, :], 0.0), axis=1, keepdims=True)
        ang = column * freq_ref[...]
        cos_t[at, :] = jnp.cos(ang)
        sin_t[at, :] = jnp.sin(ang) * sign
        return 0

    lax.fori_loop(0, SPAN // HEAD, table, 0)

    own_o.wait()
    wo_d2d.wait()
    k = 2 * p + oc
    remote(wall.at[k], wall.at[k], w_s.at[0], w_r.at[k], partner).wait_recv()
    for e in (1, 3, 2):
        for other in (0, 1):
            k = 2 * wrap(p + e) + (oc if other else c)
            there = wall.at[k, brought]
            remote(there, there, z_s.at[k], z_r.at[k], partner).wait_recv()
    for e in (1, 3, 2):
        for ss in range(RING):
            arrived(slot(wrap(p + e), ss))

    kv_sends = []
    for j in range(RING):
        at = pl.ds(j * ROWS, ROWS)
        r = jnp.dot(
            xall[RING * j : RING * j + RING].reshape(ROWS, DEPTH),
            wall[:, :, :KV_COLS].reshape(DEPTH, KV_COLS),
            preferred_element_type=F32,
        ).astype(BF16)
        for ss in range(RING):
            ykv[ss, at, :] = r[:, ss * HEAD : (ss + 1) * HEAD]
        for d in (2, 1, 3):
            ss = wrap(s + d)
            copy = remote(
                ykv.at[ss, at], ykv_in.at[s, at], ykv_s.at[j, d], ykv_r.at[j, s], device(p, ss)
            )
            copy.start()
            kv_sends.append(copy)

    q_sends = [[], [], []]

    def queries(j):
        r = jnp.dot(
            xall[:, CUT * j : CUT * j + CUT].reshape(CHUNK, DEPTH),
            wall[:, :, KV_COLS:].reshape(DEPTH, Q_COLS),
            preferred_element_type=F32,
        ).astype(BF16)
        for ss in range(RING):
            yq[j, ss] = r[:, ss * 2 * HEAD : (ss + 1) * 2 * HEAD]

    def send_queries(j):
        for d in (2, 1, 3):
            ss = wrap(s + d)
            copy = remote(yq.at[j, ss], yq_in.at[j, s], yq_s.at[j, d], yq_r.at[j, s], device(p, ss))
            copy.start()
            q_sends[j].append(copy)

    queries(0)
    send_queries(0)
    queries(1)
    queries(2)
    for copy in kv_sends:
        copy.wait_send()
    send_queries(1)

    for j in range(RING):
        at = pl.ds(j * ROWS, ROWS)
        total = ykv[s, at, :].astype(F32)
        for d in (1, 2, 3):
            ss = wrap(s + d)
            remote(
                ykv.at[ss, at], ykv_in.at[ss, at], ykv_s.at[j, d], ykv_r.at[j, ss], partner
            ).wait_recv()
            total += ykv_in[ss, at, :].astype(F32)
        whole = total.astype(BF16).astype(F32)
        turned = whole * cos_t[at, :] + pltpu.roll(whole, HEAD // 2, 1) * sin_t[at, :]
        kv[c, at, :] = jnp.where(first, turned, whole).astype(BF16)
        copy = remote(kv.at[c, at], kv.at[c, at], kv_s.at[j], kv_r.at[j], partner)
        copy.start()
        sends.append(copy)
    for copy in q_sends[0]:
        copy.wait_send()
    send_queries(2)
    for j in range(RING):
        at = pl.ds(j * ROWS, ROWS)
        remote(kv.at[oc, at], kv.at[oc, at], kv_s.at[j], kv_r.at[j], partner).wait_recv()

    def attend(j):
        for d in (1, 2, 3):
            ss = wrap(s + d)
            remote(yq.at[j, ss], yq_in.at[j, ss], yq_s.at[j, d], yq_r.at[j, ss], partner).wait_recv()
        for b in range(RING):
            rows = pl.ds(b * ROWS // 3, ROWS // 3)
            total = yq[j, s, rows, :].astype(F32)
            for d in (1, 2, 3):
                total += yq_in[j, wrap(s + d), rows, :].astype(F32)
            cos = jnp.concatenate(
                [cos_t[pl.ds(ROWS * b + TOK * i + CUT * j, CUT), :] for i in range(RING)], axis=0
            )
            sin = jnp.concatenate(
                [sin_t[pl.ds(ROWS * b + TOK * i + CUT * j, CUT), :] for i in range(RING)], axis=0
            )
            q = jnp.concatenate(
                [
                    v * cos + pltpu.roll(v, HEAD // 2, 1) * sin
                    for v in (total[:, :HEAD], total[:, HEAD:])
                ],
                axis=0,
            ).astype(BF16)
            keys = -(-(b + 1) * ROWS // HEAD) * HEAD
            scores = lax.dot_general(
                q, kv[0, :keys, :], (((1,), (1,)), ((), ())), preferred_element_type=F32
            )
            row = lax.broadcasted_iota(jnp.int32, (2 * ROWS // 3, keys), 0) % (ROWS // 3)
            row = ROWS * b + TOK * (row // CUT) + CUT * j + row % CUT
            col = lax.broadcasted_iota(jnp.int32, (2 * ROWS // 3, keys), 1)
            scores = jnp.where(col <= row, scores, -jnp.inf)
            top = jnp.max(scores, axis=1, keepdims=True)
            expo = jnp.exp2((scores - top) * EXP_SCALE)
            norm = jnp.sum(expo, axis=1, keepdims=True)
            head = jnp.dot(expo.astype(BF16), kv[1, :keys, :], preferred_element_type=F32) / norm
            hbuf[c, j, rows, :] = jnp.concatenate(
                [head[: ROWS // 3], head[ROWS // 3 :]], axis=1
            ).astype(BF16)
        copy = remote(hbuf.at[c, j], hbuf.at[c, j], h_s.at[j], h_r.at[j], partner)
        copy.start()
        sends.append(copy)

    def project(k):
        j, cols = k // 2, pl.ds((k % 2) * WIDE, WIDE)
        if k % 2 == 0:
            remote(hbuf.at[oc, j], hbuf.at[oc, j], h_s.at[j], h_r.at[j], partner).wait_recv()
        r = jnp.dot(hbuf[0, j], wo2[0, :, cols], preferred_element_type=F32)
        r += jnp.dot(hbuf[1, j], wo2[1, :, cols], preferred_element_type=F32)
        r = r.astype(BF16)
        for n in range(RING * RING):
            i, b = n // RING, n % RING
            obuf[k, jnp.where(first, b, i), jnp.where(first, i, b)] = r[CUT * n : CUT * n + CUT]
        far = wrap(p + 2)
        for d, i in ((1, 0), (3, 1)):
            copy = remote(
                obuf.at[k, far, pl.ds(2 * i, 2)], f_in.at[k, i], f_s.at[k, i], f_r.at[k, i],
                device(wrap(p + d), s),
            )
            copy.start()
            sends.append(copy)

    def fold(k):
        for d, i in ((1, 0), (3, 1)):
            near = wrap(p + d)
            remote(f_in.at[k, i], f_in.at[k, i], f_s.at[k, i], f_r.at[k, i], partner).wait_recv()
            half = pl.ds(2 * i, 2)
            obuf[k, near, half] = (
                obuf[k, near, half].astype(F32) + f_in[k, i].astype(F32)
            ).astype(BF16)
            copy = remote(
                obuf.at[k, near], o1_in.at[k, i], o1_s.at[k, i], o1_r.at[k, i], device(near, s)
            )
            copy.start()
            sends.append(copy)

    def combine(k):
        total = obuf[k, p].astype(F32)
        for i in range(2):
            remote(o1_in.at[k, i], o1_in.at[k, i], o1_s.at[k, i], o1_r.at[k, i], partner).wait_recv()
            total += o1_in[k, i].astype(F32)
        o1_sum[k] = total.astype(BF16)
        for d in (2, 1, 3):
            ss = wrap(s + d)
            copy = remote(
                o1_sum.at[k, ss], o2_in.at[k, s], o2_s.at[k, d], o2_r.at[k, s], device(p, ss)
            )
            copy.start()
            sends.append(copy)

    attend(0)
    attend(1)
    project(0)
    project(1)
    attend(2)
    project(2)
    fold(0)
    project(3)
    fold(1)
    project(4)
    fold(2)
    combine(0)
    project(5)
    fold(3)
    combine(1)
    fold(4)
    combine(2)
    fold(5)
    for k in (3, 4, 5):
        combine(k)

    def finish(k):
        total = o1_sum[k, s].astype(F32)
        for d in (1, 2, 3):
            ss = wrap(s + d)
            remote(o1_sum.at[k, 0], o2_in.at[k, ss], o2_s.at[k, d], o2_r.at[k, ss], partner).wait_recv()
            total += o2_in[k, ss].astype(F32)
        return total

    done = [finish(k) for k in range(6)]
    total = jnp.concatenate(
        [jnp.concatenate([done[2 * j], done[2 * j + 1]], axis=1) for j in range(3)], axis=0
    )
    low, high = total[: TOK // 2], total[TOK // 2 :]
    fin_out[...] = jnp.where(first, high, low).astype(BF16)
    fin_d2d = remote(fin_out, fin_in, d2d_s.at[2], d2d_r.at[2], partner)
    fin_d2d.start()
    out_ref[:, pl.ds(pl.multiple_of(c * HALF, HALF), HALF)] = jnp.where(first, low, high).astype(BF16)

    for copy in sends + q_sends[1] + q_sends[2]:
        copy.wait_send()
    fin_d2d.wait()
    out_ref[:, pl.ds(pl.multiple_of(oc * HALF, HALF), HALF)] = fin_in[...]


def shards(hidden_in, query_weight, key_weight, value_projection_weight, output_weight, head_order, positions):
    half = np.float32(ROPE_BASE) ** (
        np.float32(-2.0) * np.arange(HEAD // 2, dtype=np.float32) / np.float32(HEAD)
    )
    freq = jnp.asarray(np.concatenate([half, half])[None, :])
    vmem, dma = pltpu.VMEM, pltpu.SemaphoreType.DMA
    any_spec = pl.BlockSpec(memory_space=pl.ANY)
    vmem_spec = pl.BlockSpec(memory_space=vmem)
    return pl.pallas_call(
        kernel,
        out_shape=jax.ShapeDtypeStruct((TOK // 2, FEAT), BF16),
        in_specs=[any_spec] * 5 + [pl.BlockSpec(memory_space=pltpu.SMEM), vmem_spec, vmem_spec],
        out_specs=vmem_spec,
        scratch_shapes=[
            vmem((2, TOK // 2, FEAT), BF16),
            vmem((RING, TOK, DEPTH), BF16),
            vmem((RING * RING, TOK, DEPTH), BF16),
            vmem((HEADS, W_ROWS, HEAD), BF16),
            vmem((2, W_ROWS, 1024), BF16),
            vmem((2 * RING, W_ROWS, KV_COLS + Q_COLS), BF16),
            vmem((2 * RING, W_ROWS, KV_COLS + Q_COLS), BF16),
            vmem((2, 2 * HEAD, HALF), BF16),
            vmem((8, HEAD), jnp.int32),
            pltpu.SMEM((8, HEAD), jnp.int32),
            vmem((SPAN, HEAD), F32),
            vmem((SPAN, HEAD), F32),
            vmem((RING, SPAN, HEAD), BF16),
            vmem((RING, SPAN, HEAD), BF16),
            vmem((3, RING, CHUNK, 2 * HEAD), BF16),
            vmem((3, RING, CHUNK, 2 * HEAD), BF16),
            vmem((2, SPAN, HEAD), BF16),
            vmem((2, 3, CHUNK, 2 * HEAD), BF16),
            vmem((6, RING, RING, CUT, WIDE), BF16),
            vmem((6, 2, 2, CUT, WIDE), BF16),
            vmem((6, 2, RING, CUT, WIDE), BF16),
            vmem((6, RING, CUT, WIDE), BF16),
            vmem((6, RING, CUT, WIDE), BF16),
            vmem((TOK // 2, HALF), BF16),
            vmem((TOK // 2, HALF), BF16),
            dma((6,)), dma((3,)), dma((3,)),
            dma((2 * RING,)), dma((2 * RING,)), dma((2 * RING,)), dma((2 * RING,)),
            dma((RING,)), dma((RING * RING,)), dma((RING * RING,)),
            dma((RING, RING)), dma((RING, RING)), dma((3, RING)), dma((3, RING)),
            dma((RING,)), dma((RING,)), dma((3,)), dma((3,)),
            dma((6, 2)), dma((6, 2)), dma((6, 2)), dma((6, 2)), dma((6, RING)), dma((6, RING)),
        ],
        compiler_params=pltpu.CompilerParams(
            collective_id=0, has_side_effects=True, vmem_limit_bytes=56 << 20
        ),
        cost_estimate=pl.CostEstimate(flops=6 << 30, bytes_accessed=8 << 20, transcendentals=1 << 20),
    )(hidden_in, query_weight, key_weight, value_projection_weight, output_weight, head_order, positions, freq)


def solution(mesh):
    return jax.shard_map(
        shards,
        mesh=mesh,
        in_specs=(
            P(("replica", "tensor"), None),
            P("tensor", None),
            P("tensor", None),
            P("tensor", None),
            P("tensor", None),
            P(),
            P("replica"),
        ),
        out_specs=P(("replica", "tensor"), None),
        check_vma=False,
    )
```

time: 95.3 us -> 84.9 us (0.89)
  the two profiles are of different devices: /device:TPU:9 before, /device:TPU:1 now
where the time goes in v2:
time: 84.9 us; the launch traced here: 84.7 us
  Pallas kernels  83.1 us (98%)
  local copies, waits for them, and re-layouts  1.62 us (2%)
    pallas_call x1, Pallas kernels, shards(): pl.pallas_call(kernel, out_shape=jax.ShapeDtypeStruct((TOK // 2, FEAT), B...  83.1 us

profile of v2, /device:TPU:1, one launch (start us, length us, event | category | flops | bytes accessed | tf_op | source)
XLA Modules:
  0.0 84.7 jit_solution(2524251702027984703)
XLA Ops:
  0.0 83.1 %shard_map.82 = bf16[24,4096]{1,0:T(8,128)(2,1)} custom-call(bf16[24,4096]{1,0:T(8,128)(2,1)} %x_hbm.1, bf16[128,8192]{1,0:T(8,128)(2,1)} %wq_hbm.1, bf16[128,1024]{1,0:T(8,128)(2,1)} %wk_hbm.1, bf16[128,1024]{1,0:T(8,128)(2,1)} %wv_hbm.1, bf16[256,4096]{1,0:T(8,128)(2,1)} %wo_hbm.1, s32[64]{0:T(128)} %order_ref.1, s32[768]{0:T(1024)} %pos_ref.1, ...), custom_call_target="tpu_custom_call" | custom-call | flops 6442450944 | bytes 8388608 | tf_op jit(solution)/shard_map/pallas_call | solution.py:458
  83.1 1.6 %copy.10 = bf16[24,4096]{1,0:T(8,128)(2,1)} copy(bf16[24,4096]{1,0:T(8,128)(2,1)} %shard_map.82) | data formatting | bytes 393216

commit v3 on v2

--- a/solution.py
+++ b/solution.py
@@ -15,8 +15,6 @@
 RING = 4
 TOK = 48
 ROWS = RING * TOK
-CUT = 16
-CHUNK = RING * RING * CUT
 SPAN = RING * ROWS
 FEAT = 4096
 DEPTH = FEAT // RING
@@ -24,6 +22,7 @@
 Q_COLS = RING * 2 * HEAD
 HALF = FEAT // 2
 WIDE = HALF // 2
+PART = HALF // RING
 HEADS = 64
 W_ROWS = 128
 ROPE_BASE = 1000000.0
@@ -36,7 +35,7 @@
     xpair, xs, xall, wq, wkv, wsend, wall, wo2, inv_v, inv_s, cos_t, sin_t,
     ykv, ykv_in, yq, yq_in, kv, hbuf, obuf, f_in, o1_in, o1_sum, o2_in, fin_out, fin_in,
     loc_sem, d2d_s, d2d_r, w_s, w_r, z_s, z_r, x1_s, x2_s, x_r, ykv_s, ykv_r, yq_s, yq_r,
-    kv_s, kv_r, h_s, h_r, f_s, f_r, o1_s, o1_r, o2_s, o2_r,
+    kv_s, kv_r, h_s, h_r, f_s, f_r, o1_s, o1_r, o2_s, o2_r, fin_s, fin_r,
 ):
     t = lax.axis_index("tensor")
     z = lax.axis_index("replica")
@@ -84,6 +83,11 @@
     greet(t, -1)
     greet(partner)
 
+    @pl.when(first)
+    def _():
+        for d in range(1, RING):
+            greet(8 * wrap(y + d) + 2 * x + 1)
+
     own_x = pltpu.make_async_copy(x_hbm, xpair.at[c], loc_sem.at[0])
     own_q = pltpu.make_async_copy(wq, wq, loc_sem.at[1])
     own_k = pltpu.make_async_copy(wk_hbm, wkv.at[0], loc_sem.at[2])
@@ -112,7 +116,7 @@
     to_scalars = pltpu.make_async_copy(inv_v, inv_s, loc_sem.at[5])
     to_scalars.start()
 
-    pl.semaphore_wait(barrier, 12)
+    pl.semaphore_wait(barrier, 12 + 3 * c)
 
     x_d2d = remote(x_hbm, xpair.at[c], d2d_s.at[0], d2d_r.at[0], partner)
     x_d2d.start()
@@ -151,11 +155,12 @@
                 place.at[rows], wall.at[2 * pcc + c, rows],
                 w_s.at[RING * other + d], w_r.at[2 * pcc + c], dev,
             )
-            copy.start()
-            sends.append(copy)
-
-    for d in (1, 3, 2):
-        weights(0, d)
+            sends.append(copy)
+            return copy
+
+    near = [weights(other, d) for d in (1, 3) for other in (0, 1)]
+    for copy in near:
+        copy.start()
 
     own_x.wait()
     remote(x_hbm, xpair.at[oc], d2d_s.at[0], d2d_r.at[0], partner).wait_recv()
@@ -179,9 +184,8 @@
             copy.start()
             sends.append(copy)
 
-    for d in (1, 3, 2):
-        weights(1, d)
-    weights(1, 0)
+    far = [weights(other, 2) for other in (0, 1)]
+    weights(1, 0).start()
     weights(0, 0)
     x_d2d.wait_send()
     wo_d2d = remote(
@@ -212,12 +216,6 @@
             )
             copy.start()
             sends.append(copy)
-
-    from_plane(1)
-    from_plane(3)
-    for d in range(RING):
-        forward(d)
-    from_plane(2)
 
     eye = lax.broadcasted_iota(jnp.int32, (HEAD, HEAD), 0) == lax.broadcasted_iota(
         jnp.int32, (HEAD, HEAD), 1
@@ -235,6 +233,16 @@
 
     lax.fori_loop(0, SPAN // HEAD, table, 0)
 
+    for copy in near:
+        copy.wait_send()
+        sends.remove(copy)
+    for copy in far:
+        copy.start()
+    from_plane(1)
+    from_plane(3)
+    for d in range(RING):
+        forward(d)
+    from_plane(2)
     own_o.wait()
     wo_d2d.wait()
     k = 2 * p + oc
@@ -248,203 +256,220 @@
         for ss in range(RING):
             arrived(slot(wrap(p + e), ss))
 
-    kv_sends = []
-    for j in range(RING):
-        at = pl.ds(j * ROWS, ROWS)
+    q_sends = []
+
+    def partial(i):
+        at = pl.ds(i * ROWS, ROWS)
         r = jnp.dot(
-            xall[RING * j : RING * j + RING].reshape(ROWS, DEPTH),
-            wall[:, :, :KV_COLS].reshape(DEPTH, KV_COLS),
+            xall[RING * i : RING * i + RING].reshape(ROWS, DEPTH),
+            wall[...].reshape(DEPTH, KV_COLS + Q_COLS),
             preferred_element_type=F32,
         ).astype(BF16)
         for ss in range(RING):
             ykv[ss, at, :] = r[:, ss * HEAD : (ss + 1) * HEAD]
+            yq[i, ss] = r[:, KV_COLS + ss * 2 * HEAD : KV_COLS + (ss + 1) * 2 * HEAD]
+
+    def send_kv(i):
+        at = pl.ds(i * ROWS, ROWS)
         for d in (2, 1, 3):
             ss = wrap(s + d)
             copy = remote(
-                ykv.at[ss, at], ykv_in.at[s, at], ykv_s.at[j, d], ykv_r.at[j, s], device(p, ss)
-            )
-            copy.start()
-            kv_sends.append(copy)
-
-    q_sends = [[], [], []]
-
-    def queries(j):
-        r = jnp.dot(
-            xall[:, CUT * j : CUT * j + CUT].reshape(CHUNK, DEPTH),
-            wall[:, :, KV_COLS:].reshape(DEPTH, Q_COLS),
-            preferred_element_type=F32,
-        ).astype(BF16)
-        for ss in range(RING):
-            yq[j, ss] = r[:, ss * 2 * HEAD : (ss + 1) * 2 * HEAD]
-
-    def send_queries(j):
+                ykv.at[ss, at], ykv_in.at[s, at], ykv_s.at[i, d], ykv_r.at[i, s], device(p, ss)
+            )
+            copy.start()
+            sends.append(copy)
+
+    def send_q(i):
+        group = []
         for d in (2, 1, 3):
             ss = wrap(s + d)
-            copy = remote(yq.at[j, ss], yq_in.at[j, s], yq_s.at[j, d], yq_r.at[j, s], device(p, ss))
-            copy.start()
-            q_sends[j].append(copy)
-
-    queries(0)
-    send_queries(0)
-    queries(1)
-    queries(2)
-    for copy in kv_sends:
-        copy.wait_send()
-    send_queries(1)
-
-    for j in range(RING):
-        at = pl.ds(j * ROWS, ROWS)
+            copy = remote(yq.at[i, ss], yq_in.at[i, s], yq_s.at[i, d], yq_r.at[i, s], device(p, ss))
+            copy.start()
+            group.append(copy)
+        q_sends.append(group)
+
+    def sent_q(i):
+        for copy in q_sends[i]:
+            copy.wait_send()
+
+    def gather_kv(i):
+        at = pl.ds(i * ROWS, ROWS)
         total = ykv[s, at, :].astype(F32)
         for d in (1, 2, 3):
             ss = wrap(s + d)
             remote(
-                ykv.at[ss, at], ykv_in.at[ss, at], ykv_s.at[j, d], ykv_r.at[j, ss], partner
+                ykv.at[ss, at], ykv_in.at[ss, at], ykv_s.at[i, d], ykv_r.at[i, ss], partner
             ).wait_recv()
             total += ykv_in[ss, at, :].astype(F32)
         whole = total.astype(BF16).astype(F32)
         turned = whole * cos_t[at, :] + pltpu.roll(whole, HEAD // 2, 1) * sin_t[at, :]
         kv[c, at, :] = jnp.where(first, turned, whole).astype(BF16)
-        copy = remote(kv.at[c, at], kv.at[c, at], kv_s.at[j], kv_r.at[j], partner)
+        copy = remote(kv.at[c, at], kv.at[c, at], kv_s.at[i], kv_r.at[i], partner)
         copy.start()
         sends.append(copy)
-    for copy in q_sends[0]:
-        copy.wait_send()
-    send_queries(2)
-    for j in range(RING):
-        at = pl.ds(j * ROWS, ROWS)
-        remote(kv.at[oc, at], kv.at[oc, at], kv_s.at[j], kv_r.at[j], partner).wait_recv()
-
-    def attend(j):
+
+    def attend(i):
+        at = pl.ds(i * ROWS, ROWS)
+        remote(kv.at[oc, at], kv.at[oc, at], kv_s.at[i], kv_r.at[i], partner).wait_recv()
+        total = yq[i, s].astype(F32)
         for d in (1, 2, 3):
             ss = wrap(s + d)
-            remote(yq.at[j, ss], yq_in.at[j, ss], yq_s.at[j, d], yq_r.at[j, ss], partner).wait_recv()
-        for b in range(RING):
-            rows = pl.ds(b * ROWS // 3, ROWS // 3)
-            total = yq[j, s, rows, :].astype(F32)
-            for d in (1, 2, 3):
-                total += yq_in[j, wrap(s + d), rows, :].astype(F32)
-            cos = jnp.concatenate(
-                [cos_t[pl.ds(ROWS * b + TOK * i + CUT * j, CUT), :] for i in range(RING)], axis=0
-            )
-            sin = jnp.concatenate(
-                [sin_t[pl.ds(ROWS * b + TOK * i + CUT * j, CUT), :] for i in range(RING)], axis=0
-            )
-            q = jnp.concatenate(
-                [
-                    v * cos + pltpu.roll(v, HEAD // 2, 1) * sin
-                    for v in (total[:, :HEAD], total[:, HEAD:])
-                ],
-                axis=0,
-            ).astype(BF16)
-            keys = -(-(b + 1) * ROWS // HEAD) * HEAD
+            remote(yq.at[i, ss], yq_in.at[i, ss], yq_s.at[i, d], yq_r.at[i, ss], partner).wait_recv()
+            total += yq_in[i, ss].astype(F32)
+        keys = (i + 1) * ROWS
+        row = i * ROWS + lax.broadcasted_iota(jnp.int32, (ROWS, keys), 0)
+        seen = lax.broadcasted_iota(jnp.int32, (ROWS, keys), 1) <= row
+        for h in range(2):
+            v = total[:, h * HEAD : (h + 1) * HEAD]
+            q = (v * cos_t[at, :] + pltpu.roll(v, HEAD // 2, 1) * sin_t[at, :]).astype(BF16)
             scores = lax.dot_general(
                 q, kv[0, :keys, :], (((1,), (1,)), ((), ())), preferred_element_type=F32
             )
-            row = lax.broadcasted_iota(jnp.int32, (2 * ROWS // 3, keys), 0) % (ROWS // 3)
-            row = ROWS * b + TOK * (row // CUT) + CUT * j + row % CUT
-            col = lax.broadcasted_iota(jnp.int32, (2 * ROWS // 3, keys), 1)
-            scores = jnp.where(col <= row, scores, -jnp.inf)
+            scores = jnp.where(seen, scores, -jnp.inf)
             top = jnp.max(scores, axis=1, keepdims=True)
             expo = jnp.exp2((scores - top) * EXP_SCALE)
             norm = jnp.sum(expo, axis=1, keepdims=True)
             head = jnp.dot(expo.astype(BF16), kv[1, :keys, :], preferred_element_type=F32) / norm
-            hbuf[c, j, rows, :] = jnp.concatenate(
-                [head[: ROWS // 3], head[ROWS // 3 :]], axis=1
-            ).astype(BF16)
-        copy = remote(hbuf.at[c, j], hbuf.at[c, j], h_s.at[j], h_r.at[j], partner)
+            hbuf[c, i, :, h * HEAD : (h + 1) * HEAD] = head.astype(BF16)
+        copy = remote(hbuf.at[c, i], hbuf.at[c, i], h_s.at[i], h_r.at[i], partner)
         copy.start()
         sends.append(copy)
 
-    def project(k):
-        j, cols = k // 2, pl.ds((k % 2) * WIDE, WIDE)
-        if k % 2 == 0:
-            remote(hbuf.at[oc, j], hbuf.at[oc, j], h_s.at[j], h_r.at[j], partner).wait_recv()
-        r = jnp.dot(hbuf[0, j], wo2[0, :, cols], preferred_element_type=F32)
-        r += jnp.dot(hbuf[1, j], wo2[1, :, cols], preferred_element_type=F32)
-        r = r.astype(BF16)
-        for n in range(RING * RING):
-            i, b = n // RING, n % RING
-            obuf[k, jnp.where(first, b, i), jnp.where(first, i, b)] = r[CUT * n : CUT * n + CUT]
-        far = wrap(p + 2)
-        for d, i in ((1, 0), (3, 1)):
+    def project(i):
+        remote(hbuf.at[oc, i], hbuf.at[oc, i], h_s.at[i], h_r.at[i], partner).wait_recv()
+        far_place = wrap(p + 2)
+        for w in range(2):
+            cols = pl.ds(w * WIDE, WIDE)
+            r = jnp.dot(hbuf[0, i], wo2[0, :, cols], preferred_element_type=F32)
+            r += jnp.dot(hbuf[1, i], wo2[1, :, cols], preferred_element_type=F32)
+            r = r.astype(BF16)
+            for b in range(RING):
+                for v in range(2):
+                    g = 2 * w + v
+                    obuf[i, jnp.where(first, b, g), jnp.where(first, g, b)] = r[
+                        b * TOK : (b + 1) * TOK, v * PART : (v + 1) * PART
+                    ]
+        for d, w in ((1, 0), (3, 1)):
             copy = remote(
-                obuf.at[k, far, pl.ds(2 * i, 2)], f_in.at[k, i], f_s.at[k, i], f_r.at[k, i],
+                obuf.at[i, far_place, pl.ds(2 * w, 2)], f_in.at[i, w], f_s.at[i, w], f_r.at[i, w],
                 device(wrap(p + d), s),
             )
             copy.start()
             sends.append(copy)
 
-    def fold(k):
-        for d, i in ((1, 0), (3, 1)):
-            near = wrap(p + d)
-            remote(f_in.at[k, i], f_in.at[k, i], f_s.at[k, i], f_r.at[k, i], partner).wait_recv()
-            half = pl.ds(2 * i, 2)
-            obuf[k, near, half] = (
-                obuf[k, near, half].astype(F32) + f_in[k, i].astype(F32)
+    def fold(i):
+        for d, w in ((1, 0), (3, 1)):
+            place, half = wrap(p + d), pl.ds(2 * w, 2)
+            remote(f_in.at[i, w], f_in.at[i, w], f_s.at[i, w], f_r.at[i, w], partner).wait_recv()
+            obuf[i, place, half] = (
+                obuf[i, place, half].astype(F32) + f_in[i, w].astype(F32)
             ).astype(BF16)
             copy = remote(
-                obuf.at[k, near], o1_in.at[k, i], o1_s.at[k, i], o1_r.at[k, i], device(near, s)
-            )
-            copy.start()
-            sends.append(copy)
-
-    def combine(k):
-        total = obuf[k, p].astype(F32)
-        for i in range(2):
-            remote(o1_in.at[k, i], o1_in.at[k, i], o1_s.at[k, i], o1_r.at[k, i], partner).wait_recv()
-            total += o1_in[k, i].astype(F32)
-        o1_sum[k] = total.astype(BF16)
+                obuf.at[i, place], o1_in.at[i, w], o1_s.at[i, w], o1_r.at[i, w], device(place, s)
+            )
+            copy.start()
+            sends.append(copy)
+
+    def combine(i):
+        total = obuf[i, p].astype(F32)
+        for w in range(2):
+            remote(o1_in.at[i, w], o1_in.at[i, w], o1_s.at[i, w], o1_r.at[i, w], partner).wait_recv()
+            total += o1_in[i, w].astype(F32)
+        o1_sum[i] = total.astype(BF16)
         for d in (2, 1, 3):
             ss = wrap(s + d)
             copy = remote(
-                o1_sum.at[k, ss], o2_in.at[k, s], o2_s.at[k, d], o2_r.at[k, s], device(p, ss)
-            )
-            copy.start()
-            sends.append(copy)
-
+                o1_sum.at[i, ss], o2_in.at[i, s], o2_s.at[i, d], o2_r.at[i, s], device(p, ss)
+            )
+            copy.start()
+            sends.append(copy)
+
+    def final(i, core):
+        return remote(
+            fin_out.at[i, core], fin_in.at[c, y], fin_s.at[i, core], fin_r.at[c, y],
+            8 * i + 2 * x + core,
+        )
+
+    def finish(i):
+        total = o1_sum[i, s].astype(F32)
+        for d in (1, 2, 3):
+            ss = wrap(s + d)
+            remote(o1_sum.at[i, 0], o2_in.at[i, ss], o2_s.at[i, d], o2_r.at[i, ss], partner).wait_recv()
+            total += o2_in[i, ss].astype(F32)
+        for core in range(2):
+            rows = total[core * (TOK // 2) : (core + 1) * (TOK // 2)].astype(BF16)
+            fin_out[i, core] = rows
+            mine_now = jnp.logical_and(y == i, c == core)
+
+            @pl.when(mine_now)
+            def _(rows=rows):
+                fin_in[c, y] = rows
+
+            @pl.when(jnp.logical_not(mine_now))
+            def _(core=core):
+                final(i, core).start()
+
+    partial(0)
+    send_kv(0)
+    send_q(0)
+    partial(1)
+    send_kv(1)
+    send_q(1)
+    partial(2)
+    send_kv(2)
+    partial(3)
+    send_kv(3)
+    gather_kv(0)
+    sent_q(0)
+    send_q(2)
+    gather_kv(1)
+    sent_q(1)
+    send_q(3)
     attend(0)
+    gather_kv(2)
     attend(1)
+    gather_kv(3)
     project(0)
     project(1)
     attend(2)
+    fold(0)
+    attend(3)
+    fold(1)
     project(2)
-    fold(0)
     project(3)
-    fold(1)
-    project(4)
+    combine(0)
     fold(2)
-    combine(0)
-    project(5)
+    combine(1)
     fold(3)
-    combine(1)
-    fold(4)
+    finish(0)
     combine(2)
-    fold(5)
-    for k in (3, 4, 5):
-        combine(k)
-
-    def finish(k):
-        total = o1_sum[k, s].astype(F32)
-        for d in (1, 2, 3):
-            ss = wrap(s + d)
-            remote(o1_sum.at[k, 0], o2_in.at[k, ss], o2_s.at[k, d], o2_r.at[k, ss], partner).wait_recv()
-            total += o2_in[k, ss].astype(F32)
-        return total
-
-    done = [finish(k) for k in range(6)]
-    total = jnp.concatenate(
-        [jnp.concatenate([done[2 * j], done[2 * j + 1]], axis=1) for j in range(3)], axis=0
-    )
-    low, high = total[: TOK // 2], total[TOK // 2 :]
-    fin_out[...] = jnp.where(first, high, low).astype(BF16)
-    fin_d2d = remote(fin_out, fin_in, d2d_s.at[2], d2d_r.at[2], partner)
-    fin_d2d.start()
-    out_ref[:, pl.ds(pl.multiple_of(c * HALF, HALF), HALF)] = jnp.where(first, low, high).astype(BF16)
-
-    for copy in sends + q_sends[1] + q_sends[2]:
+    finish(1)
+    combine(3)
+    finish(2)
+    finish(3)
+
+    sent_q(2)
+    sent_q(3)
+    for copy in sends:
         copy.wait_send()
-    fin_d2d.wait()
-    out_ref[:, pl.ds(pl.multiple_of(oc * HALF, HALF), HALF)] = fin_in[...]
+    for i in range(RING):
+        for core in range(2):
+
+            @pl.when(jnp.logical_or(y != i, c != core))
+            def _(i=i, core=core):
+                final(i, core).wait_send()
+
+    for cc in range(2):
+        for yy in range(RING):
+
+            @pl.when(jnp.logical_or(y != yy, c != cc))
+            def _(cc=cc, yy=yy):
+                remote(
+                    fin_out.at[0, 0], fin_in.at[cc, yy], fin_s.at[0, 0], fin_r.at[cc, yy], partner
+                ).wait_recv()
+
+            col = cc * HALF + yy * PART
+            out_ref[:, col : col + PART] = fin_in[cc, yy]
 
 
 def shards(hidden_in, query_weight, key_weight, value_projection_weight, output_weight, head_order, positions):
@@ -475,23 +500,24 @@
             vmem((SPAN, HEAD), F32),
             vmem((RING, SPAN, HEAD), BF16),
             vmem((RING, SPAN, HEAD), BF16),
-            vmem((3, RING, CHUNK, 2 * HEAD), BF16),
-            vmem((3, RING, CHUNK, 2 * HEAD), BF16),
+            vmem((RING, RING, ROWS, 2 * HEAD), BF16),
+            vmem((RING, RING, ROWS, 2 * HEAD), BF16),
             vmem((2, SPAN, HEAD), BF16),
-            vmem((2, 3, CHUNK, 2 * HEAD), BF16),
-            vmem((6, RING, RING, CUT, WIDE), BF16),
-            vmem((6, 2, 2, CUT, WIDE), BF16),
-            vmem((6, 2, RING, CUT, WIDE), BF16),
-            vmem((6, RING, CUT, WIDE), BF16),
-            vmem((6, RING, CUT, WIDE), BF16),
-            vmem((TOK // 2, HALF), BF16),
-            vmem((TOK // 2, HALF), BF16),
-            dma((6,)), dma((3,)), dma((3,)),
+            vmem((2, RING, ROWS, 2 * HEAD), BF16),
+            vmem((RING, RING, RING, TOK, PART), BF16),
+            vmem((RING, 2, 2, TOK, PART), BF16),
+            vmem((RING, 2, RING, TOK, PART), BF16),
+            vmem((RING, RING, TOK, PART), BF16),
+            vmem((RING, RING, TOK, PART), BF16),
+            vmem((RING, 2, TOK // 2, PART), BF16),
+            vmem((2, RING, TOK // 2, PART), BF16),
+            dma((6,)), dma((2,)), dma((2,)),
             dma((2 * RING,)), dma((2 * RING,)), dma((2 * RING,)), dma((2 * RING,)),
             dma((RING,)), dma((RING * RING,)), dma((RING * RING,)),
-            dma((RING, RING)), dma((RING, RING)), dma((3, RING)), dma((3, RING)),
-            dma((RING,)), dma((RING,)), dma((3,)), dma((3,)),
-            dma((6, 2)), dma((6, 2)), dma((6, 2)), dma((6, 2)), dma((6, RING)), dma((6, RING)),
+            dma((RING, RING)), dma((RING, RING)), dma((RING, RING)), dma((RING, RING)),
+            dma((RING,)), dma((RING,)), dma((RING,)), dma((RING,)),
+            dma((RING, 2)), dma((RING, 2)), dma((RING, 2)), dma((RING, 2)),
+            dma((RING, RING)), dma((RING, RING)), dma((RING, 2)), dma((2, RING)),
         ],
         compiler_params=pltpu.CompilerParams(
             collective_id=0, has_side_effects=True, vmem_limit_bytes=56 << 20

time: 84.9 us -> 82.6 us (0.973)
  the two profiles are of different devices: /device:TPU:1 before, /device:TPU:25 now
where the time goes in v3:
time: 82.6 us; the launch traced here: 82.5 us
  Pallas kernels  80.8 us (98%)
  local copies, waits for them, and re-layouts  1.62 us (2%)
    pallas_call x1, Pallas kernels, shards(): pl.pallas_call(kernel, out_shape=jax.ShapeDtypeStruct((TOK // 2, FEAT), B...  80.8 us

profile of v3, /device:TPU:25, one launch (start us, length us, event | category | flops | bytes accessed | tf_op | source)
XLA Modules:
  0.0 82.5 jit_solution(11906406540821910348)
XLA Ops:
  0.0 80.8 %shard_map.82 = bf16[24,4096]{1,0:T(8,128)(2,1)} custom-call(bf16[24,4096]{1,0:T(8,128)(2,1)} %x_hbm.1, bf16[128,8192]{1,0:T(8,128)(2,1)} %wq_hbm.1, bf16[128,1024]{1,0:T(8,128)(2,1)} %wk_hbm.1, bf16[128,1024]{1,0:T(8,128)(2,1)} %wv_hbm.1, bf16[256,4096]{1,0:T(8,128)(2,1)} %wo_hbm.1, s32[64]{0:T(128)} %order_ref.1, s32[768]{0:T(1024)} %pos_ref.1, ...), custom_call_target="tpu_custom_call" | custom-call | flops 6442450944 | bytes 8388608 | tf_op jit(solution)/shard_map/pallas_call | solution.py:483
  80.8 1.6 %copy.10 = bf16[24,4096]{1,0:T(8,128)(2,1)} copy(bf16[24,4096]{1,0:T(8,128)(2,1)} %shard_map.82) | data formatting | bytes 393216

commit v4 on v3

--- a/solution.py
+++ b/solution.py
@@ -34,7 +34,7 @@
     out_ref,
     xpair, xs, xall, wq, wkv, wsend, wall, wo2, inv_v, inv_s, cos_t, sin_t,
     ykv, ykv_in, yq, yq_in, kv, hbuf, obuf, f_in, o1_in, o1_sum, o2_in, fin_out, fin_in,
-    loc_sem, d2d_s, d2d_r, w_s, w_r, z_s, z_r, x1_s, x2_s, x_r, ykv_s, ykv_r, yq_s, yq_r,
+    loc_sem, d2d_s, d2d_r, w_s, w_r, e_s, z_s, z_r, x1_s, x2_s, x_r, ykv_s, ykv_r, yq_s, yq_r,
     kv_s, kv_r, h_s, h_r, f_s, f_r, o1_s, o1_r, o2_s, o2_r, fin_s, fin_r,
 ):
     t = lax.axis_index("tensor")
@@ -45,6 +45,7 @@
     p, s = jnp.where(first, x, y), jnp.where(first, y, x)
     oc = 1 - c
     part = z % 2
+    beyond = {1: z + 1 < planes, -1: z > 0}
 
     def wrap(v):
         return lax.rem(v + 8, RING)
@@ -79,9 +80,13 @@
         greet(ring)
         greet(ring + 1 - 2 * c)
         greet(device(p, wrap(s + d)))
-    greet(t, 1)
-    greet(t, -1)
     greet(partner)
+    for dz in (1, -1):
+
+        @pl.when(beyond[dz])
+        def _(dz=dz):
+            greet(t, dz)
+
 
     @pl.when(first)
     def _():
@@ -116,7 +121,8 @@
     to_scalars = pltpu.make_async_copy(inv_v, inv_s, loc_sem.at[5])
     to_scalars.start()
 
-    pl.semaphore_wait(barrier, 12 + 3 * c)
+    ends = jnp.where(beyond[1], 0, 1) + jnp.where(beyond[-1], 0, 1)
+    pl.semaphore_wait(barrier, 12 - ends + 3 * c)
 
     x_d2d = remote(x_hbm, xpair.at[c], d2d_s.at[0], d2d_r.at[0], partner)
     x_d2d.start()
@@ -125,7 +131,7 @@
     own_v.wait()
     own_q.wait()
 
-    sends = []
+    sends, extra, forwards = [], [], []
     half_rows = W_ROWS // 2
     moved = pl.ds(pl.multiple_of(part * half_rows, half_rows), half_rows)
     brought = pl.ds(pl.multiple_of((1 - part) * half_rows, half_rows), half_rows)
@@ -136,27 +142,39 @@
         pcc = jnp.where(cc_first, x, y)
         pp = wrap(pcc + d)
         own = other == 0 and d == 0
+        place = wall.at[2 * p + c] if own else wsend.at[RING * other + d]
+
+        def fill(rows):
+            def step(ss, _):
+                tt = jnp.where(cc_first, 8 * ss + 2 * pp, 8 * pp + 2 * ss + 1)
+                group = pl.multiple_of((tt // 4) * HEAD, HEAD)
+                place[rows, pl.ds(pl.multiple_of(ss * HEAD, HEAD), HEAD)] = wkv[
+                    cc, rows, pl.ds(group, HEAD)
+                ]
+                for i in range(2):
+                    at = pl.multiple_of(KV_COLS + (2 * ss + i) * HEAD, HEAD)
+                    place[rows, pl.ds(at, HEAD)] = wq[inv_s[0, 2 * tt + i], rows]
+                return 0
+
+            lax.fori_loop(0, RING, step, 0)
+
+        def copy_of(rows, leave, arrive):
+            dev = jnp.where(cc_first, 8 * y + 2 * pp, 8 * pp + 2 * x + 1)
+            return remote(
+                place.at[rows], wall.at[2 * pcc + c, rows],
+                leave.at[RING * other + d], arrive.at[2 * pcc + c], dev,
+            )
+
         rows = moved if d else pl.ds(0, W_ROWS)
-        place = wall.at[2 * p + c] if own else wsend.at[RING * other + d]
-
-        def fill(ss, _):
-            tt = jnp.where(cc_first, 8 * ss + 2 * pp, 8 * pp + 2 * ss + 1)
-            group = pl.multiple_of((tt // 4) * HEAD, HEAD)
-            place[rows, pl.ds(pl.multiple_of(ss * HEAD, HEAD), HEAD)] = wkv[cc, rows, pl.ds(group, HEAD)]
-            for i in range(2):
-                at = pl.multiple_of(KV_COLS + (2 * ss + i) * HEAD, HEAD)
-                place[rows, pl.ds(at, HEAD)] = wq[inv_s[0, 2 * tt + i], rows]
-            return 0
-
-        lax.fori_loop(0, RING, fill, 0)
-        if not own:
-            dev = jnp.where(cc_first, 8 * y + 2 * pp, 8 * pp + 2 * x + 1)
-            copy = remote(
-                place.at[rows], wall.at[2 * pcc + c, rows],
-                w_s.at[RING * other + d], w_r.at[2 * pcc + c], dev,
-            )
-            sends.append(copy)
-            return copy
+        fill(rows)
+        if own:
+            return None
+        copy = copy_of(rows, w_s, w_r)
+        sends.append(copy)
+        if d in (1, 3):
+            alone = jnp.logical_not(beyond[1 if other else -1])
+            extra.append((alone, fill, copy_of(brought, e_s, z_r)))
+        return copy
 
     near = [weights(other, d) for d in (1, 3) for other in (0, 1)]
     for copy in near:
@@ -202,9 +220,15 @@
             k = 2 * wrap(p + e) + (oc if other else c)
             here = wall.at[k, moved]
             remote(here, here, w_s.at[0], w_r.at[k], partner).wait_recv()
-            copy = remote(here, here, z_s.at[k], z_r.at[k], t, -1 if other else 1)
-            copy.start()
-            sends.append(copy)
+            dz = -1 if other else 1
+            copy = remote(here, here, z_s.at[k], z_r.at[k], t, dz)
+            pl.when(beyond[dz])(copy.start)
+            forwards.append((beyond[dz], copy))
+            if e == 2:
+                last = z == (planes - 2 if other else 1)
+                copy = remote(here, here, e_s.at[RING * other + e], z_r.at[k], t, -dz)
+                pl.when(last)(copy.start)
+                forwards.append((last, copy))
 
     def forward(d):
         m = slot(p, wrap(s + d))
@@ -238,6 +262,13 @@
         sends.remove(copy)
     for copy in far:
         copy.start()
+    for alone, fill, copy in extra:
+
+        @pl.when(alone)
+        def _(fill=fill, copy=copy):
+            fill(brought)
+            copy.start()
+
     from_plane(1)
     from_plane(3)
     for d in range(RING):
@@ -349,6 +380,15 @@
                     obuf[i, jnp.where(first, b, g), jnp.where(first, g, b)] = r[
                         b * TOK : (b + 1) * TOK, v * PART : (v + 1) * PART
                     ]
+        if i == RING - 1:
+            for d, w in ((2, 2), (1, 0), (3, 1)):
+                place = wrap(p + d)
+                copy = remote(
+                    obuf.at[i, place], o1_in.at[i, w], o1_s.at[i, w], o1_r.at[i, w], device(place, s)
+                )
+                copy.start()
+                sends.append(copy)
+            return
         for d, w in ((1, 0), (3, 1)):
             copy = remote(
                 obuf.at[i, far_place, pl.ds(2 * w, 2)], f_in.at[i, w], f_s.at[i, w], f_r.at[i, w],
@@ -372,7 +412,7 @@
 
     def combine(i):
         total = obuf[i, p].astype(F32)
-        for w in range(2):
+        for w in range(3 if i == RING - 1 else 2):
             remote(o1_in.at[i, w], o1_in.at[i, w], o1_s.at[i, w], o1_r.at[i, w], partner).wait_recv()
             total += o1_in[i, w].astype(F32)
         o1_sum[i] = total.astype(BF16)
@@ -413,11 +453,11 @@
     send_kv(0)
     send_q(0)
     partial(1)
+    partial(2)
+    partial(3)
     send_kv(1)
     send_q(1)
-    partial(2)
     send_kv(2)
-    partial(3)
     send_kv(3)
     gather_kv(0)
     sent_q(0)
@@ -426,21 +466,20 @@
     sent_q(1)
     send_q(3)
     attend(0)
+    attend(1)
+    project(0)
     gather_kv(2)
-    attend(1)
+    project(1)
     gather_kv(3)
-    project(0)
-    project(1)
+    fold(0)
     attend(2)
-    fold(0)
+    fold(1)
     attend(3)
-    fold(1)
     project(2)
+    combine(0)
     project(3)
-    combine(0)
     fold(2)
     combine(1)
-    fold(3)
     finish(0)
     combine(2)
     finish(1)
@@ -452,6 +491,10 @@
     sent_q(3)
     for copy in sends:
         copy.wait_send()
+    for alone, _, copy in extra:
+        pl.when(alone)(copy.wait_send)
+    for active, copy in forwards:
+        pl.when(active)(copy.wait_send)
     for i in range(RING):
         for core in range(2):
 
@@ -506,17 +549,17 @@
             vmem((2, RING, ROWS, 2 * HEAD), BF16),
             vmem((RING, RING, RING, TOK, PART), BF16),
             vmem((RING, 2, 2, TOK, PART), BF16),
-            vmem((RING, 2, RING, TOK, PART), BF16),
+            vmem((RING, 3, RING, TOK, PART), BF16),
             vmem((RING, RING, TOK, PART), BF16),
             vmem((RING, RING, TOK, PART), BF16),
             vmem((RING, 2, TOK // 2, PART), BF16),
             vmem((2, RING, TOK // 2, PART), BF16),
             dma((6,)), dma((2,)), dma((2,)),
-            dma((2 * RING,)), dma((2 * RING,)), dma((2 * RING,)), dma((2 * RING,)),
+            dma((2 * RING,)), dma((2 * RING,)), dma((2 * RING,)), dma((2 * RING,)), dma((2 * RING,)),
             dma((RING,)), dma((RING * RING,)), dma((RING * RING,)),
             dma((RING, RING)), dma((RING, RING)), dma((RING, RING)), dma((RING, RING)),
             dma((RING,)), dma((RING,)), dma((RING,)), dma((RING,)),
-            dma((RING, 2)), dma((RING, 2)), dma((RING, 2)), dma((RING, 2)),
+            dma((RING, 2)), dma((RING, 2)), dma((RING, 3)), dma((RING, 3)),
             dma((RING, RING)), dma((RING, RING)), dma((RING, 2)), dma((2, RING)),
         ],
         compiler_params=pltpu.CompilerParams(

time: 82.6 us -> 81 us (0.981)
  the two profiles are of different devices: /device:TPU:25 before, /device:TPU:1 now
where the time goes in v4:
time: 81 us; the launch traced here: 80.3 us
  Pallas kernels  78.7 us (97%)
  local copies, waits for them, and re-layouts  1.62 us (2%)
    pallas_call x1, Pallas kernels, shards(): pl.pallas_call(kernel, out_shape=jax.ShapeDtypeStruct((TOK // 2, FEAT), B...  78.7 us

profile of v4, /device:TPU:1, one launch (start us, length us, event | category | flops | bytes accessed | tf_op | source)
XLA Modules:
  0.0 80.3 jit_solution(4202856873430352600)
XLA Ops:
  0.0 78.7 %shard_map.82 = bf16[24,4096]{1,0:T(8,128)(2,1)} custom-call(bf16[24,4096]{1,0:T(8,128)(2,1)} %x_hbm.1, bf16[128,8192]{1,0:T(8,128)(2,1)} %wq_hbm.1, bf16[128,1024]{1,0:T(8,128)(2,1)} %wk_hbm.1, bf16[128,1024]{1,0:T(8,128)(2,1)} %wv_hbm.1, bf16[256,4096]{1,0:T(8,128)(2,1)} %wo_hbm.1, s32[64]{0:T(128)} %order_ref.1, s32[768]{0:T(1024)} %pos_ref.1, ...), custom_call_target="tpu_custom_call" | custom-call | flops 6442450944 | bytes 8388608 | tf_op jit(solution)/shard_map/pallas_call | solution.py:526
  78.7 1.6 %copy.10 = bf16[24,4096]{1,0:T(8,128)(2,1)} copy(bf16[24,4096]{1,0:T(8,128)(2,1)} %shard_map.82) | data formatting | bytes 393216

commit v5 on v4

--- a/solution.py
+++ b/solution.py
@@ -525,7 +525,7 @@
     vmem_spec = pl.BlockSpec(memory_space=vmem)
     return pl.pallas_call(
         kernel,
-        out_shape=jax.ShapeDtypeStruct((TOK // 2, FEAT), BF16),
+        out_shape=pltpu.VMEM((TOK // 2, FEAT), BF16),
         in_specs=[any_spec] * 5 + [pl.BlockSpec(memory_space=pltpu.SMEM), vmem_spec, vmem_spec],
         out_specs=vmem_spec,
         scratch_shapes=[

time: 81 us -> 79.4 us (0.980)
  local copies, waits for them, and re-layouts: 1.62 us -> 0.68 us
    unnamed x1, local copies, waits for them, and re-layouts: 1.62 us -> 0.68 us
where the time goes in v5:
time: 79.4 us; the launch traced here: 78.7 us
  Pallas kernels  78 us (98%)
    pallas_call x1, Pallas kernels, shards(): pl.pallas_call(kernel, out_shape=pltpu.VMEM((TOK // 2, FEAT), BF16), in_s...  78 us

profile of v5, /device:TPU:1, one launch (start us, length us, event | category | flops | bytes accessed | tf_op | source)
XLA Modules:
  0.0 78.7 jit_solution(11796816667132676994)
XLA Ops:
  0.0 78.0 %shard_map.82 = bf16[24,4096]{1,0:T(8,128)(2,1)S(1)} custom-call(bf16[24,4096]{1,0:T(8,128)(2,1)} %x_hbm.1, bf16[128,8192]{1,0:T(8,128)(2,1)} %wq_hbm.1, bf16[128,1024]{1,0:T(8,128)(2,1)} %wk_hbm.1, bf16[128,1024]{1,0:T(8,128)(2,1)} %wv_hbm.1, bf16[256,4096]{1,0:T(8,128)(2,1)} %wo_hbm.1, s32[64]{0:T(128)} %order_ref.1, s32[768]{0:T(1024)} %pos_ref.1, ...), custom_call_target="tpu_custom_call" | custom-call | flops 6442450944 | bytes 8388608 | tf_op jit(solution)/shard_map/pallas_call | solution.py:526
  78.0 0.7 copy.10

commit v6 on v5

--- a/solution.py
+++ b/solution.py
@@ -30,11 +30,11 @@
 
 
 def kernel(
-    x_hbm, wq_hbm, wk_hbm, wv_hbm, wo_hbm, order_ref, pos_ref, freq_ref,
+    x_hbm, wq_hbm, wk_hbm, wv_hbm, wo_hbm, order_ref, pos_hbm, freq_hbm,
     out_ref,
     xpair, xs, xall, wq, wkv, wsend, wall, wo2, inv_v, inv_s, cos_t, sin_t,
     ykv, ykv_in, yq, yq_in, kv, hbuf, obuf, f_in, o1_in, o1_sum, o2_in, fin_out, fin_in,
-    loc_sem, d2d_s, d2d_r, w_s, w_r, e_s, z_s, z_r, x1_s, x2_s, x_r, ykv_s, ykv_r, yq_s, yq_r,
+    pos_ref, freq_ref, loc_sem, d2d_s, d2d_r, w_s, w_r, e_s, z_s, z_r, x1_s, x2_s, x_r, ykv_s, ykv_r, yq_s, yq_r,
     kv_s, kv_r, h_s, h_r, f_s, f_r, o1_s, o1_r, o2_s, o2_r, fin_s, fin_r,
 ):
     t = lax.axis_index("tensor")
@@ -111,6 +111,10 @@
     lax.fori_loop(0, HEADS, load_head, 0, unroll=8)
     own_x.start()
     own_o.start()
+    own_pos = pltpu.make_async_copy(pos_hbm, pos_ref, loc_sem.at[6])
+    own_freq = pltpu.make_async_copy(freq_hbm, freq_ref, loc_sem.at[7])
+    own_pos.start()
+    own_freq.start()
 
     lane = lax.broadcasted_iota(jnp.int32, (8, HEAD), 1)
 
@@ -255,6 +259,8 @@
         sin_t[at, :] = jnp.sin(ang) * sign
         return 0
 
+    own_pos.wait()
+    own_freq.wait()
     lax.fori_loop(0, SPAN // HEAD, table, 0)
 
     for copy in near:
@@ -526,7 +532,7 @@
     return pl.pallas_call(
         kernel,
         out_shape=pltpu.VMEM((TOK // 2, FEAT), BF16),
-        in_specs=[any_spec] * 5 + [pl.BlockSpec(memory_space=pltpu.SMEM), vmem_spec, vmem_spec],
+        in_specs=[any_spec] * 5 + [pl.BlockSpec(memory_space=pltpu.SMEM), any_spec, any_spec],
         out_specs=vmem_spec,
         scratch_shapes=[
             vmem((2, TOK // 2, FEAT), BF16),
@@ -554,7 +560,9 @@
             vmem((RING, RING, TOK, PART), BF16),
             vmem((RING, 2, TOK // 2, PART), BF16),
             vmem((2, RING, TOK // 2, PART), BF16),
-            dma((6,)), dma((2,)), dma((2,)),
+            vmem((SPAN,), jnp.int32),
+            vmem((1, HEAD), F32),
+            dma((8,)), dma((2,)), dma((2,)),
             dma((2 * RING,)), dma((2 * RING,)), dma((2 * RING,)), dma((2 * RING,)), dma((2 * RING,)),
             dma((RING,)), dma((RING * RING,)), dma((RING * RING,)),
             dma((RING, RING)), dma((RING, RING)), dma((RING, RING)), dma((RING, RING)),

time: 79.4 us -> 79.4 us (level)
  no operation moved by 1% of the time
where the time goes in v6:
time: 79.4 us; the launch traced here: 78.7 us
  Pallas kernels  78 us (98%)
    pallas_call x1, Pallas kernels, shards(): pl.pallas_call(kernel, out_shape=pltpu.VMEM((TOK // 2, FEAT), BF16), in_s...  78 us

profile of v6, /device:TPU:1, one launch (start us, length us, event | category | flops | bytes accessed | tf_op | source)
XLA Modules:
  0.0 78.7 jit_solution(2298863808630925134)
XLA Ops:
  0.0 78.0 %shard_map.82 = bf16[24,4096]{1,0:T(8,128)(2,1)S(1)} custom-call(bf16[24,4096]{1,0:T(8,128)(2,1)} %x_hbm.1, bf16[128,8192]{1,0:T(8,128)(2,1)} %wq_hbm.1, bf16[128,1024]{1,0:T(8,128)(2,1)} %wk_hbm.1, bf16[128,1024]{1,0:T(8,128)(2,1)} %wv_hbm.1, bf16[256,4096]{1,0:T(8,128)(2,1)} %wo_hbm.1, s32[64]{0:T(128)} %order_ref.1, s32[768]{0:T(1024)} %pos_hbm.1, ...), custom_call_target="tpu_custom_call" | custom-call | flops 6442450944 | bytes 8388608 | tf_op jit(solution)/shard_map/pallas_call | solution.py:532
  78.0 0.7 copy.10
